TPU v7x, 32 devices: a whole 2x2x4 slice. The times are simulated.
32 devices in a mesh: space: 8 (over y, x, core), tm: 4 (over z).
Axes of the slice: x: 2, y: 2, z: 4, core: 2. Of those that a mesh axis runs over, the one named last changes fastest.
Arguments:
- latents: bfloat16 [16, 16, 240, 320], P('tm', 'space'), may hold values from -6 to 6
- cotangent: bfloat16 [16, 16, 240, 320], P('tm', 'space'), may hold values from -6 to 6
- conv_weight: bfloat16 [3, 3, 320, 320], replicated, may hold values from -0.109375 to 0.109375
- query_weight: bfloat16 [320, 320], replicated, may hold values from -3 to 3
- key_weight: bfloat16 [320, 320], replicated, may hold values from -3 to 3
- value_weight: bfloat16 [320, 320], replicated, may hold values from -0.3125 to 0.3125
- out_weight: bfloat16 [320, 320], replicated, may hold values from -0.3125 to 0.3125
Outputs:
- grad_input: bfloat16 [16, 16, 240, 320], P('tm', 'space')
- grad_conv: float32 [3, 3, 320, 320], replicated
- grad_query: float32 [320, 320], replicated
- grad_key: float32 [320, 320], replicated
- grad_value: float32 [320, 320], replicated
- grad_out: float32 [320, 320], replicated
All inputs are finite; a program needn't handle non-finite values.
Results may differ from a plain program's by a relative error of at most 0.011.
The roundings to bfloat16 on the way count: a program that leaves them out, or rounds other values in their place, can miss the bound.
Values may be sent and summed in bfloat16 or wider, within the bound.
A program may use at most 128 MiB of HBM per device.

v0:
```python
import jax
import jax.numpy as jnp
from jax import lax
from jax.sharding import PartitionSpec as P

HEAD_DIM = 64


def extended(cells, sides, width):
    for axis, dim in sides:
        count = lax.axis_size(axis)
        ends = count - 1
        head = lax.slice_in_dim(cells, 0, width, axis=dim)
        tail = lax.slice_in_dim(cells, cells.shape[dim] - width, cells.shape[dim], axis=dim)
        cells = jnp.concatenate(
            [
                lax.ppermute(tail, axis, [(i, (i + 1) % count) for i in range(ends)]),
                cells,
                lax.ppermute(head, axis, [((i + 1) % count, i) for i in range(ends)]),
            ],
            axis=dim,
        )
    return cells


def project(arr, weight):
    shape = arr.shape
    flat = jnp.dot(arr.reshape(-1, shape[-1]), weight, preferred_element_type=jnp.float32)
    return flat.reshape(shape[:-1] + (weight.shape[1],))


def contract(left, right):
    chans = left.shape[-1]
    return lax.dot_general(
        left.reshape(-1, chans),
        right.reshape(-1, right.shape[-1]),
        (((0,), (0,)), ((), ())),
        preferred_element_type=jnp.float32,
    )


def attend(query_rows, key_rows, value_rows, out_grad):
    frames, pixels, chans = query_rows.shape
    heads = chans // HEAD_DIM
    scale = HEAD_DIM ** (-0.5)

    def split(arr):
        return arr.reshape(frames, pixels, heads, HEAD_DIM)

    qsplit, ksplit, vsplit, gsplit = (
        split(query_rows),
        split(key_rows),
        split(value_rows),
        split(out_grad),
    )
    scores = (
        jnp.einsum("fwhd,gwhd->whfg", qsplit, ksplit, preferred_element_type=jnp.float32) * scale
    )
    prob = jax.nn.softmax(scores, axis=-1)
    prob_low = prob.astype(jnp.bfloat16)
    attended = jnp.einsum(
        "whfg,gwhd->fwhd", prob_low, vsplit, preferred_element_type=jnp.float32
    ).astype(jnp.bfloat16)
    dprob = jnp.einsum("fwhd,gwhd->whfg", gsplit, vsplit, preferred_element_type=jnp.float32)
    dscore = prob * (dprob - jnp.sum(prob * dprob, axis=-1, keepdims=True))
    dscore = (dscore * scale).astype(jnp.bfloat16)
    query_grad = jnp.einsum(
        "whfg,gwhd->fwhd", dscore, ksplit, preferred_element_type=jnp.float32
    ).astype(jnp.bfloat16)
    key_grad = jnp.einsum(
        "whfg,fwhd->gwhd", dscore, qsplit, preferred_element_type=jnp.float32
    ).astype(jnp.bfloat16)
    value_grad = jnp.einsum(
        "whfg,fwhd->gwhd", prob_low, gsplit, preferred_element_type=jnp.float32
    ).astype(jnp.bfloat16)
    shape = (frames, pixels, chans)
    return (
        attended.reshape(shape),
        query_grad.reshape(shape),
        key_grad.reshape(shape),
        value_grad.reshape(shape),
    )


def as_columns(arr):
    frames, rows, cols, chans = arr.shape
    return arr.reshape(frames, rows * cols, chans)


def on_device(latents, cotangent, conv_weight, query_weight, key_weight, value_weight, out_weight):
    frames, rows, cols, chans = latents.shape
    with_rows = extended(latents, (("space", 1),), 1)
    padded = jnp.pad(with_rows, ((0, 0), (0, 0), (1, 1), (0, 0)))
    total = latents.astype(jnp.float32)
    for row_off in range(3):
        for col_off in range(3):
            total = total + project(
                padded[:, row_off : row_off + rows, col_off : col_off + cols],
                conv_weight[row_off, col_off],
            )
    hidden = total.astype(jnp.bfloat16)
    whole_count = frames * lax.axis_size("tm") * rows * lax.axis_size("space") * cols
    norm = 1.0 / jnp.sqrt(jnp.float32(whole_count))
    hidden_cols, grad_cols = (
        lax.all_to_all(hidden, "tm", split_axis=2, concat_axis=0, tiled=True),
        lax.all_to_all(cotangent, "tm", split_axis=2, concat_axis=0, tiled=True),
    )
    col_shape = hidden_cols.shape
    hidden_flat = as_columns(hidden_cols)
    grad_flat = as_columns(grad_cols)
    queries = project(hidden_flat, query_weight).astype(jnp.bfloat16)
    keys_all = project(hidden_flat, key_weight).astype(jnp.bfloat16)
    values_all = project(hidden_flat, value_weight).astype(jnp.bfloat16)
    out_grad = project(grad_flat, out_weight.T).astype(jnp.bfloat16)
    attended, query_grad, key_grad, value_grad = attend(queries, keys_all, values_all, out_grad)
    grad_out = contract(attended, grad_flat)
    grad_query = contract(hidden_flat, query_grad)
    grad_key = contract(hidden_flat, key_grad)
    grad_value = contract(hidden_flat, value_grad)
    attn_cols = (
        project(query_grad, query_weight.T)
        + project(key_grad, key_weight.T)
        + project(value_grad, value_weight.T)
    ).astype(jnp.bfloat16)
    attn_grad = lax.all_to_all(
        attn_cols.reshape(col_shape), "tm", split_axis=0, concat_axis=2, tiled=True
    )
    hidden_grad = (cotangent.astype(jnp.float32) + attn_grad.astype(jnp.float32)).astype(
        jnp.bfloat16
    )
    kernel_rows = []
    for row_off in range(3):
        kernel_cols = []
        for col_off in range(3):
            kernel_cols.append(
                contract(padded[:, row_off : row_off + rows, col_off : col_off + cols], hidden_grad)
            )
        kernel_rows.append(jnp.stack(kernel_cols))
    grad_conv = jnp.stack(kernel_rows)
    grad_with_rows = extended(hidden_grad, (("space", 1),), 1)
    grad_padded = jnp.pad(grad_with_rows, ((0, 0), (0, 0), (1, 1), (0, 0)))
    result = hidden_grad.astype(jnp.float32)
    for row_off in range(3):
        for col_off in range(3):
            piece = grad_padded[
                :, 2 - row_off : 2 - row_off + rows, 2 - col_off : 2 - col_off + cols
            ]
            result = result + project(piece, conv_weight[row_off, col_off].T)
    grad_input = result.astype(jnp.bfloat16)
    grad_conv, grad_query, grad_key, grad_value, grad_out = lax.psum(
        (grad_conv, grad_query, grad_key, grad_value, grad_out), ("space", "tm")
    )
    return (
        grad_input,
        grad_conv * norm,
        grad_query * norm,
        grad_key * norm,
        grad_value * norm,
        grad_out * norm,
    )


def solution(mesh):
    in_specs = (P("tm", "space", None, None), P("tm", "space", None, None), P(), P(), P(), P(), P())
    out_specs = (P("tm", "space", None, None), P(), P(), P(), P(), P())
    return jax.shard_map(
        on_device, mesh=mesh, in_specs=in_specs, out_specs=out_specs, check_vma=False
    )
```

profile of v0, /device:TPU:0, one launch (start us, length us, event | category | flops | bytes accessed | tf_op | source)
XLA Modules:
  0.0 462.2 jit_solution(4574876135501568268)
XLA Ops:
  7.2 2.6 fusion.126
  9.8 3.2 collective-permute-start
  14.4 2.2 copy.173
  16.6 5.7 %all-to-all-start.1 = ((bf16[4,2,240,320]{3,0,1,2:T(4,128)(2,1)}), bf16[4,2,240,320]{3,0,1,2:T(4,128)(2,1)}, u32[]{:S(2)}, u32[]{:S(2)}) async-start(bf16[4,2,240,320]{3,0,1,2:T(4,128)(2,1)} %copy.173), calls=%async_computation.1 | async-start | bytes 2949120 | tf_op jit(solution)/shard_map/all_to_all | solution.py:106
  22.3 1.8 fusion.79
  24.1 3.1 select_maximum_fusion.2
  33.3 1.6 constant_dynamic-update-slice_fusion.2
  37.1 2.8 add_convert_fusion.3
  39.8 5.0 %copy.164 = bf16[4,2,240,320]{3,1,0,2:T(2,128)(2,1)} copy(bf16[4,2,240,320]{2,3,1,0:T(8,128)(2,1)} %add_convert_fusion.3) | data formatting | bytes 2457600 | tf_op jit(solution)/shard_map/convert_element_type | solution.py:101
  44.8 13.5 %all-to-all-done.1 = bf16[4,2,240,320]{3,0,1,2:T(4,128)(2,1)} async-done(((bf16[4,2,240,320]{3,0,1,2:T(4,128)(2,1)}), bf16[4,2,240,320]{3,0,1,2:T(4,128)(2,1)}, u32[]{:S(2)}, u32[]{:S(2)}) %all-to-all-start.1) | async-done | bytes 1228832 | tf_op jit(solution)/shard_map/all_to_all | solution.py:106
  58.3 3.7 all-to-all-start
  62.0 2.5 copy.174
  65.7 1.5 copy.209
  67.2 8.4 %copy.245 = bf16[4,4,2,60,320]{3,2,4,1,0:T(2,128)(2,1)} copy(bf16[4,4,2,60,320]{4,2,3,0,1:T(2,128)(2,1)} %bitcast.289) | data formatting | bytes 2457600 | tf_op jit(solution)/shard_map/dot_general | solution.py:28
  75.6 3.5 reshape_reshape.32
  79.1 5.4 %reshape.188 = bf16[16,120,320]{1,2,0:T(8,128)(2,1)} reshape(bf16[4,4,2,60,320]{3,2,4,1,0:T(2,128)(2,1)} %copy.245) | data formatting | bytes 2457600 | tf_op jit(solution)/shard_map/dot_general | solution.py:28
  84.5 3.2 convolution_convert_fusion.1
  87.7 5.6 %copy.179 = bf16[16,120,5,64]{3,0,2,1:T(8,128)(2,1)} copy(bf16[16,120,5,64]{1,3,2,0:T(8,128)(2,1)} %bitcast.294) | data formatting | bytes 2457600 | tf_op jit(solution)/shard_map/reshape | solution.py:48
  93.3 4.1 all-to-all-done
  98.6 6.2 %copy.258 = bf16[4,4,2,60,320]{3,2,4,1,0:T(2,128)(2,1)} copy(bf16[4,4,2,60,320]{4,2,1,3,0:T(2,128)(2,1)S(1)} %bitcast.286) | data formatting | bytes 2457600 | tf_op jit(solution)/shard_map/dot_general | solution.py:28
  104.7 4.6 reshape.189
  109.3 1.9 convolution_convert_fusion.2
  111.3 5.7 %copy.171 = bf16[16,120,5,64]{3,0,2,1:T(8,128)(2,1)} copy(bf16[16,120,5,64]{1,3,2,0:T(8,128)(2,1)} %bitcast.296) | data formatting | bytes 2457600 | tf_op jit(solution)/shard_map/reshape | solution.py:48
  116.9 1.9 convolution_convert_fusion.3
  118.9 5.8 %copy.181 = bf16[16,120,5,64]{3,0,2,1:T(8,128)(2,1)} copy(bf16[16,120,5,64]{1,3,2,0:T(8,128)(2,1)} %bitcast.297) | data formatting | bytes 2457600 | tf_op jit(solution)/shard_map/reshape | solution.py:48
  124.7 1.9 convolution_convert_fusion
  126.6 5.6 %copy.180 = bf16[16,120,5,64]{3,0,2,1:T(8,128)(2,1)} copy(bf16[16,120,5,64]{1,3,2,0:T(8,128)(2,1)} %bitcast.295) | data formatting | bytes 2457600 | tf_op jit(solution)/shard_map/reshape | solution.py:48
  132.3 7.1 %fusion.127 = (f32[120,5,16]{2,1,0:T(8,128)S(1)}, f32[120,5,16,16]{2,3,1,0:T(8,128)}) fusion(bf16[16,120,5,64]{3,0,2,1:T(8,128)(2,1)} %copy.171, bf16[16,120,5,64]{3,0,2,1:T(8,128)(2,1)} %copy.181), kind=kOutput, calls=%fused_computation.155 | convolution fusion | flops 20121616 | bytes 3110400 | tf_op jit(solution)/shard_map/sub | solution.py:59
  139.4 6.3 %fusion.128 = f32[120,5,16,16]{2,3,1,0:T(8,128)} fusion(bf16[16,120,5,64]{3,0,2,1:T(8,128)(2,1)} %copy.179, bf16[16,120,5,64]{3,0,2,1:T(8,128)(2,1)} %copy.180), kind=kOutput, calls=%fused_computation.156 | convolution fusion | flops 19660800 | bytes 3072000 | tf_op jit(solution)/shard_map/fwhd,gwhd->whfg/dot_general | solution.py:64
  145.7 2.9 convert_bitcast_fusion.1
  148.6 11.1 %convert_bitcast_fusion.2 = bf16[16,120,5,64]{3,0,2,1:T(8,128)(2,1)} fusion(bf16[16,120,5,64]{3,0,2,1:T(8,128)(2,1)} %copy.171, f32[120,5,16,16]{2,3,1,0:T(8,128)} %fusion.128, f32[120,5,16,16]{2,3,1,0:T(8,128)} %get-tuple-element.18, f32[120,5,16]{2,1,0:T(8,128)S(1)} %get-tuple-element.17), kind=kOutput, calls=%fused_computation.23 | convolution fusion | flops 21360016 | bytes 3724800 | tf_op jit(solution)/shard_map/whfg,fwhd->gwhd/dot_general | solution.py:70
  159.7 10.8 %convert_bitcast_fusion.3 = bf16[16,120,5,64]{3,0,2,1:T(8,128)(2,1)} fusion(bf16[16,120,5,64]{3,0,2,1:T(8,128)(2,1)} %copy.181, f32[120,5,16,16]{2,3,1,0:T(8,128)} %fusion.128, f32[120,5,16,16]{2,3,1,0:T(8,128)} %get-tuple-element.18, f32[120,5,16]{2,1,0:T(8,128)S(1)} %get-tuple-element.17), kind=kOutput, calls=%fused_computation.24 | convolution fusion | flops 21360016 | bytes 3724800 | tf_op jit(solution)/shard_map/whfg,gwhd->fwhd/dot_general | solution.py:67
  170.5 4.9 %copy.187 = bf16[16,120,5,64]{1,3,2,0:T(8,128)(2,1)} copy(bf16[16,120,5,64]{3,0,2,1:T(8,128)(2,1)} %convert_bitcast_fusion.1) | data formatting | bytes 2457600 | tf_op jit(solution)/shard_map/convert_element_type | solution.py:75
  175.5 6.6 %copy.205 = bf16[16,120,5,64]{1,0,3,2:T(8,128)(2,1)} copy(bf16[16,120,5,64]{3,0,2,1:T(8,128)(2,1)} %convert_bitcast_fusion.1) | data formatting | bytes 2457600 | tf_op jit(solution)/shard_map/convert_element_type | solution.py:75
  183.6 4.2 copy.185
  187.8 6.2 %copy.204 = bf16[16,120,5,64]{1,0,3,2:T(8,128)(2,1)} copy(bf16[16,120,5,64]{3,0,2,1:T(8,128)(2,1)} %convert_bitcast_fusion.2) | data formatting | bytes 2457600 | tf_op jit(solution)/shard_map/convert_element_type | solution.py:72
  194.0 4.9 %copy.183 = bf16[16,120,5,64]{1,3,2,0:T(8,128)(2,1)} copy(bf16[16,120,5,64]{3,0,2,1:T(8,128)(2,1)} %convert_bitcast_fusion.3) | data formatting | bytes 2457600 | tf_op jit(solution)/shard_map/convert_element_type | solution.py:69
  198.9 6.2 %copy.203 = bf16[16,120,5,64]{1,0,3,2:T(8,128)(2,1)} copy(bf16[16,120,5,64]{3,0,2,1:T(8,128)(2,1)} %convert_bitcast_fusion.3) | data formatting | bytes 2457600 | tf_op jit(solution)/shard_map/convert_element_type | solution.py:69
  207.4 2.0 add_convert_fusion.2
  209.4 2.1 copy.188
  211.5 2.7 copy.189
  214.2 4.3 all-to-all-start.2
  218.8 5.6 %convert_bitcast_fusion = bf16[16,120,5,64]{3,0,2,1:T(8,128)(2,1)} fusion(bf16[16,120,5,64]{3,0,2,1:T(8,128)(2,1)} %copy.180, f32[120,5,16,16]{2,3,1,0:T(8,128)} %get-tuple-element.18, f32[120,5,16]{2,1,0:T(8,128)S(1)} %copy-done.34), kind=kOutput, calls=%fused_computation.21 | convolution fusion | flops 20582400 | bytes 3110400 | tf_op jit(solution)/shard_map/whfg,gwhd->fwhd/dot_general | solution.py:61
  224.3 6.2 %copy.208 = bf16[16,120,5,64]{1,0,3,2:T(8,128)(2,1)} copy(bf16[16,120,5,64]{3,0,2,1:T(8,128)(2,1)} %convert_bitcast_fusion) | data formatting | bytes 2457600 | tf_op jit(solution)/shard_map/convert_element_type | solution.py:63
  230.5 3.8 reshape_reshape.31
  234.3 3.7 reshape_reshape.30
  238.1 1.5 reshape_reshape.12
  239.5 3.8 reshape_reshape.14
  243.3 2.4 reshape_reshape.13
  245.7 3.6 fusion.131
  249.4 1.8 fusion.130
  251.2 1.8 fusion.129
  252.9 1.6 fusion.132
  254.5 4.0 copy.190
  258.5 5.7 %copy.191 = f32[4,2,240,320]{2,3,1,0:T(8,128)} copy(f32[4,2,240,320]{3,1,2,0:T(2,128)} %bitcast.290) | data formatting | bytes 4915200 | tf_op jit(solution)/shard_map/convert_element_type | solution.py:128
  264.2 2.6 add_convert_fusion.1
  278.9 3.9 collective-permute-start.2
  283.1 2.4 pad_maximum_fusion
  285.5 1.8 fusion.77
  287.3 3.3 select_maximum_fusion
  292.4 1.9 fusion.25
  298.0 3.4 add_convert_fusion
  301.4 145.4 %all-reduce.5.cloned.1.call-done = (f32[3,3,320,320]{3,2,1,0:T(8,128)}, f32[320,320]{1,0:T(8,128)}, f32[320,320]{1,0:T(8,128)}, f32[320,320]{1,0:T(8,128)}, f32[320,320]{1,0:T(8,128)}) async-done(((f32[3,3,320,320]{3,2,1,0:T(8,128)}, f32[320,320]{1,0:T(8,128)}, f32[320,320]{1,0:T(8,128)}, f32[320,320]{1,0:T(8,128)}, f32[320,320]{1,0:T(8,128)}), (f32[3,3,320,320]{3,2,1,0:T(8,128)}, f32[320,320]{1,0:T(8,128)}, ...) | async-done | bytes 5324816 | tf_op jit(solution)/shard_map/psum | solution.py:150
  446.8 4.8 %broadcast_multiply_fusion = f32[3,3,320,320]{3,2,1,0:T(8,128)} fusion(f32[3,3,320,320]{3,2,1,0:T(8,128)} %get-tuple-element.6), kind=kLoop, calls=%fused_computation.29 | loop fusion | flops 921600 | bytes 7372800 | tf_op jit(solution)/shard_map/mul | solution.py:155
  (113 shorter events, 36.8 us)
Async XLA Ops:
  7.2 109.8 %copy-start = (bf16[320,320]{1,0:T(8,128)(2,1)S(1)}, bf16[320,320]{1,0:T(8,128)(2,1)}, u32[]{:S(2)}) copy-start(bf16[320,320]{1,0:T(8,128)(2,1)} %param.11) | copy-start | bytes 614404
  7.2 7.2 %copy-start.12 = (bf16[4,2,240,320]{2,3,1,0:T(8,128)(2,1)S(1)}, bf16[4,2,240,320]{2,3,1,0:T(8,128)(2,1)}, u32[]{:S(2)}) copy-start(bf16[4,2,240,320]{2,3,1,0:T(8,128)(2,1)} %param.8) | copy-start | bytes 3686404
  9.8 14.3 %collective-permute-start = (bf16[4,1,240,320]{2,3,1,0:T(8,128)(2,1)}, bf16[4,1,240,320]{2,3,1,0:T(8,128)(2,1)}, u32[]{:S(2)}, u32[]{:S(2)}) collective-permute-start(bf16[4,1,240,320]{2,3,1,0:T(8,128)(2,1)} %get-tuple-element.15), channel_id=1, source_target_pairs={{0,4},{4,8},{8,12},{12,16},{16,20},{20,24},{24,28},{1,5},{5,9},{9,... | collective-permute-start | bytes 1843208 | tf_op jit(solution)/shard_map/ppermute | solution.py:17
  12.9 9.3 %copy-start.4 = (bf16[4,2,240,320]{2,3,1,0:T(8,128)(2,1)S(1)}, bf16[4,2,240,320]{2,3,1,0:T(8,128)(2,1)}, u32[]{:S(2)}) copy-start(bf16[4,2,240,320]{2,3,1,0:T(8,128)(2,1)} %param.7) | copy-start | bytes 3686404
  12.9 11.2 %collective-permute-start.1 = (bf16[4,1,240,320]{2,3,1,0:T(8,128)(2,1)}, bf16[4,1,240,320]{2,3,1,0:T(8,128)(2,1)}, u32[]{:S(2)}, u32[]{:S(2)}) collective-permute-start(bf16[4,1,240,320]{2,3,1,0:T(8,128)(2,1)} %get-tuple-element.16), channel_id=1, source_target_pairs={{4,0},{8,4},{12,8},{16,12},{20,16},{24,20},{28,24},{5,1},{9,5},{13... | collective-permute-start | bytes 1843208 | tf_op jit(solution)/shard_map/ppermute | solution.py:19
  16.6 41.7 %all-to-all-start.1 = ((bf16[4,2,240,320]{3,0,1,2:T(4,128)(2,1)}), bf16[4,2,240,320]{3,0,1,2:T(4,128)(2,1)}, u32[]{:S(2)}, u32[]{:S(2)}) async-start(bf16[4,2,240,320]{3,0,1,2:T(4,128)(2,1)} %copy.173), calls=%async_computation.1 | async-start | bytes 2949120 | tf_op jit(solution)/shard_map/all_to_all | solution.py:106
  24.1 3.2 copy-start.9
  27.3 9.8 %copy-start.2 = (bf16[4,4,242,320]{2,3,1,0:T(8,128)(2,1)}, bf16[4,4,242,320]{2,3,1,0:T(8,128)(2,1)S(1)}, u32[]{:S(2)}) copy-start(bf16[4,4,242,320]{2,3,1,0:T(8,128)(2,1)S(1)} %select_maximum_fusion.2) | copy-start | bytes 7434244
  33.3 2.9 copy-start.18
  34.9 1.3 copy-start.16
  58.3 39.1 %all-to-all-start = ((bf16[4,2,240,320]{3,1,0,2:T(2,128)(2,1)}), bf16[4,2,240,320]{3,1,0,2:T(2,128)(2,1)S(1)}, u32[]{:S(2)}, u32[]{:S(2)}) async-start(bf16[4,2,240,320]{3,1,0,2:T(2,128)(2,1)} %copy.164), calls=%async_computation | async-start | bytes 2949120 | tf_op jit(solution)/shard_map/all_to_all | solution.py:105
  64.5 1.1 copy-start.7
  79.1 5.4 %copy-start.31 = (bf16[320,320]{1,0:T(8,128)(2,1)S(1)}, bf16[320,320]{1,0:T(8,128)(2,1)}, u32[]{:S(2)}) copy-start(bf16[320,320]{1,0:T(8,128)(2,1)} %param.13) | copy-start | bytes 614404
  97.5 1.1 copy-start.5
  104.7 4.6 copy-start.25
  118.9 5.8 %copy-start.26 = (bf16[320,320]{1,0:T(8,128)(2,1)S(1)}, bf16[320,320]{1,0:T(8,128)(2,1)}, u32[]{:S(2)}) copy-start(bf16[320,320]{1,0:T(8,128)(2,1)} %param.12) | copy-start | bytes 614404
  139.4 20.3 %copy-start.33 = (f32[120,5,16]{2,1,0:T(8,128)}, f32[120,5,16]{2,1,0:T(8,128)S(1)}, u32[]{:S(2)}) copy-start(f32[120,5,16]{2,1,0:T(8,128)S(1)} %get-tuple-element.17) | copy-start | bytes 115204
  139.4 6.3 %copy-start.8 = (bf16[16,120,5,64]{3,0,2,1:T(8,128)(2,1)S(1)}, bf16[16,120,5,64]{3,0,2,1:T(8,128)(2,1)}, u32[]{:S(2)}) copy-start(bf16[16,120,5,64]{3,0,2,1:T(8,128)(2,1)} %copy.179) | copy-start | bytes 3686404
  139.4 6.3 %copy-start.32 = (f32[120,5,16,16]{2,3,1,0:T(8,128)S(1)}, f32[120,5,16,16]{2,3,1,0:T(8,128)}, u32[]{:S(2)}) copy-start(f32[120,5,16,16]{2,3,1,0:T(8,128)} %get-tuple-element.18) | copy-start | bytes 1843204
  175.5 6.6 %copy-start.6 = (bf16[4,2,240,320]{3,1,0,2:T(2,128)(2,1)S(1)}, bf16[4,2,240,320]{3,1,0,2:T(2,128)(2,1)}, u32[]{:S(2)}) copy-start(bf16[4,2,240,320]{3,1,0,2:T(2,128)(2,1)} %copy-done.5) | copy-start | bytes 3686404
  205.1 1.3 copy-start.14
  206.0 1.4 copy-start.15
  211.5 7.3 %copy-start.34 = (f32[120,5,16]{2,1,0:T(8,128)S(1)}, f32[120,5,16]{2,1,0:T(8,128)}, u32[]{:S(2)}) copy-start(f32[120,5,16]{2,1,0:T(8,128)} %copy-done.33) | copy-start | bytes 115204
  214.2 40.4 %all-to-all-start.2 = ((bf16[16,2,60,320]{3,1,2,0:T(2,128)(2,1)}), bf16[16,2,60,320]{3,1,2,0:T(2,128)(2,1)}, u32[]{:S(2)}, u32[]{:S(2)}) async-start(bf16[16,2,60,320]{3,1,2,0:T(2,128)(2,1)} %copy.189), calls=%async_computation.2 | async-start | bytes 2949120 | tf_op jit(solution)/shard_map/all_to_all | solution.py:125
  218.5 228.3 %all-reduce.5.cloned.1.call-start = ((), (), s32[]{:S(2)}) async-start(), calls=%async_computation.3 | async-start | bytes 12779520 | tf_op jit(solution)/shard_map/psum | solution.py:150
  230.5 7.6 %copy-start.11 = (bf16[4,4,2,60,320]{4,3,2,1,0:T(8,128)(2,1)S(1)}, bf16[4,4,2,60,320]{4,3,2,1,0:T(8,128)(2,1)}, u32[]{:S(2)}) copy-start(bf16[4,4,2,60,320]{4,3,2,1,0:T(8,128)(2,1)} %copy.202) | copy-start | bytes 3686404
  239.5 3.8 copy-start.13
  245.7 3.6 copy-start.21
  245.7 3.6 copy-start.24
  249.4 1.8 copy-start.23
  251.1 1.8 copy-start.20
  251.1 1.8 copy-start.22
  264.2 2.7 copy-start.19
  267.0 1.7 copy-start.3
  272.2 1.5 copy-start.17
  277.6 9.7 %collective-permute-start.3 = (bf16[4,1,240,320]{2,3,1,0:T(8,128)(2,1)}, bf16[4,1,240,320]{2,3,1,0:T(8,128)(2,1)S(1)}, u32[]{:S(2)}, u32[]{:S(2)}) collective-permute-start(bf16[4,1,240,320]{2,3,1,0:T(8,128)(2,1)} %get-tuple-element.11), channel_id=1, source_target_pairs={{4,0},{8,4},{12,8},{16,12},{20,16},{24,20},{28,24},{5,1},{9,5},{13... | collective-permute-start | bytes 1843208 | tf_op jit(solution)/shard_map/ppermute | solution.py:19
  278.9 8.4 %collective-permute-start.2 = (bf16[4,1,240,320]{2,3,1,0:T(8,128)(2,1)}, bf16[4,1,240,320]{2,3,1,0:T(8,128)(2,1)}, u32[]{:S(2)}, u32[]{:S(2)}) collective-permute-start(bf16[4,1,240,320]{2,3,1,0:T(8,128)(2,1)} %get-tuple-element.12), channel_id=1, source_target_pairs={{0,4},{4,8},{8,12},{12,16},{16,20},{20,24},{24,28},{1,5},{5,9},{9,... | collective-permute-start | bytes 1843208 | tf_op jit(solution)/shard_map/ppermute | solution.py:17
  287.3 3.3 copy-start.10
  446.8 4.9 %copy-start.30 = (f32[320,320]{1,0:T(8,128)S(1)}, f32[320,320]{1,0:T(8,128)}, u32[]{:S(2)}) copy-start(f32[320,320]{1,0:T(8,128)} %get-tuple-element.10) | copy-start | bytes 1228804
  446.8 5.7 %copy-start.29 = (f32[320,320]{1,0:T(8,128)S(1)}, f32[320,320]{1,0:T(8,128)}, u32[]{:S(2)}) copy-start(f32[320,320]{1,0:T(8,128)} %get-tuple-element.9) | copy-start | bytes 1228804
  446.8 6.5 %copy-start.28 = (f32[320,320]{1,0:T(8,128)S(1)}, f32[320,320]{1,0:T(8,128)}, u32[]{:S(2)}) copy-start(f32[320,320]{1,0:T(8,128)} %get-tuple-element.8) | copy-start | bytes 1228804
  446.8 8.2 %copy-start.1 = (bf16[320,320]{1,0:T(8,128)(2,1)S(1)}, bf16[320,320]{1,0:T(8,128)(2,1)}, u32[]{:S(2)}) copy-start(bf16[320,320]{1,0:T(8,128)(2,1)} %param.11) | copy-start | bytes 614404
  451.7 2.5 copy-start.27
Sparse Core Ops, SparseCore 0:
  285.6 161.1 all-reduce.4
where the time goes:
time: 471 us; the launch traced here: 462 us
  waiting for transfers between devices  163 us (35%)
  local copies, waits for them, and re-layouts  144 us (31%)
  matrix products  96.4 us (20%)
  starting transfers between devices  23.7 us (5%)
  other arithmetic  19.8 us (4%)
  between operations  15 us (3%)
    psum x1, waiting for transfers between devices, on_device(): lax.psum((grad_conv, grad_query, grad_key, grad_value, grad_out), ('space...  145 us
    dot_general x25, matrix products, project(): jnp.dot(arr.reshape(-1, shape[-1]), weight, preferred_element_type=jnp.fl...  36.1 us
    dot_general x4, local copies, waits for them, and re-layouts, project(): jnp.dot(arr.reshape(-1, shape[-1]), weight, preferred_element_type=jnp.fl...  24.6 us
    reshape x4, local copies, waits for them, and re-layouts, split(): return arr.reshape(frames, pixels, heads, HEAD_DIM)  22.7 us
    dot_general x13, matrix products, contract(): lax.dot_general(left.reshape(-1, chans), right.reshape(-1, right.shape[-1...  16.6 us
    another operation x5, local copies, waits for them, and re-layouts, project(): arr.reshape(-1, shape[-1])  14.9 us
    all_to_all x1, waiting for transfers between devices, on_device(): lax.all_to_all(cotangent, 'tm', split_axis=2, concat_axis=0, tiled=True)  13.5 us
    convert_element_type x2, local copies, waits for them, and re-layouts, attend(): value_grad = jnp.einsum('whfg,fwhd->gwhd', prob_low, gsplit, preferred_el...  11.6 us
  transfers between devices with their start and end apart: 8, of which 3 were waited for; matrix products, arithmetic and copies ran while one was open for 23% of the time, Pallas kernels for 0%

commit v1 on v0

v1 whole, which is shorter than its diff:
```python
import functools

import jax
import jax.numpy as jnp
from jax import lax
from jax.experimental import pallas as pl
from jax.experimental.pallas import tpu as pltpu
from jax.sharding import PartitionSpec as P

HEAD_DIM = 64
PIXEL_BLOCK = 8
F32 = jnp.float32
BF16 = jnp.bfloat16
VMEM_BYTES = 50 * 1024 * 1024
MESH = pl.DeviceIdType.MESH


def call(body, out_shape, args, scratch=(), flops=0, **params):
    size = sum(a.size * a.dtype.itemsize for a in args)
    return pl.pallas_call(
        body,
        out_shape=out_shape,
        in_specs=[pl.BlockSpec(memory_space=pltpu.VMEM)] * len(args),
        out_specs=jax.tree.map(lambda _: pl.BlockSpec(memory_space=pltpu.VMEM), out_shape),
        scratch_shapes=list(scratch),
        compiler_params=pltpu.CompilerParams(vmem_limit_bytes=VMEM_BYTES, **params),
        cost_estimate=pl.CostEstimate(flops=flops, bytes_accessed=2 * size, transcendentals=0),
    )(*args)


def shape_of(shape, dtype):
    return jax.ShapeDtypeStruct(shape, dtype)


def dot(left, right, dims=((1,), (0,))):
    return lax.dot_general(left, right, (dims, ((), ())), preferred_element_type=F32)


def shifted(arr, step, rows, cols):
    total = rows * cols
    moved = pltpu.roll(arr, (-step) % total, 0)
    place = lax.broadcasted_iota(jnp.int32, arr.shape, 0)
    edge = None
    for row in range(rows):
        hit = place == (row * cols + (0 if step < 0 else cols - 1))
        edge = hit if edge is None else edge | hit
    return jnp.where(edge, 0.0, moved)


def regroup(parts, groups):
    chans = parts[0].shape[-1]
    cat = jnp.concatenate([part.reshape(-1, PIXEL_BLOCK, chans) for part in parts], axis=1)
    return cat.astype(BF16)


def regroup_kernel(cells_ref, out_ref):
    frames, rows, cols, chans = cells_ref.shape
    real = rows * cols // PIXEL_BLOCK
    parts = [cells_ref[f].reshape(rows * cols, chans).astype(F32) for f in range(frames)]
    out_ref[0:real] = regroup(parts, real)
    if out_ref.shape[0] > real:
        out_ref[real:] = jnp.zeros((out_ref.shape[0] - real,) + out_ref.shape[1:], BF16)


def conv_kernel(grouped, top_ref, cells_ref, bottom_ref, weight_ref, out_ref, ext, *scratch):
    frames, rows, cols, chans = cells_ref.shape

    def one_frame(f, carry):
        ext[0] = top_ref[f]
        ext[1 : rows + 1] = cells_ref[f]
        ext[rows + 1] = bottom_ref[f]
        total = cells_ref[f].reshape(rows * cols, chans).astype(F32)
        for b in range(3):
            part = None
            for a in range(3):
                piece = ext[a : a + rows].reshape(rows * cols, chans)
                prod = dot(piece, weight_ref[3 * a + b])
                part = prod if part is None else part + prod
            total = total + (part if b == 1 else shifted(part, b - 1, rows, cols))
        if grouped:
            scratch[0][f] = total
        else:
            out_ref[f] = total.astype(BF16).reshape(rows, cols, chans)
        return carry

    lax.fori_loop(0, frames, one_frame, 0)
    if grouped:
        real = rows * cols // PIXEL_BLOCK
        out_ref[0:real] = regroup([scratch[0][f] for f in range(frames)], real)
        if out_ref.shape[0] > real:
            out_ref[real:] = jnp.zeros((out_ref.shape[0] - real,) + out_ref.shape[1:], BF16)


def convolve(top, cells, bottom, weight, groups=None):
    frames, rows, cols, chans = cells.shape
    scratch = [pltpu.VMEM((rows + 2, cols, chans), BF16)]
    if groups is None:
        out = shape_of(cells.shape, BF16)
    else:
        out = shape_of((groups, frames * PIXEL_BLOCK, chans), BF16)
        scratch.append(pltpu.VMEM((frames, rows * cols, chans), F32))
    return call(
        functools.partial(conv_kernel, groups is not None),
        out,
        (top, cells, bottom, weight),
        scratch,
        flops=18 * cells.size * chans,
    )


def attend_kernel(
    hid, cot, wq, wk, wv, wot, wqt, wkt, wvt, cols_o, att_o, qg_o, kg_o, vg_o, q_s, k_s, v_s, g_s
):
    sources, groups, span, chans = hid.shape
    heads = chans // HEAD_DIM
    scale = HEAD_DIM ** (-0.5)
    size = sources * span
    flat = groups * span

    def project(t, carry):
        h = hid[t].reshape(flat, chans)
        for ref, w in ((q_s, wq), (k_s, wk), (v_s, wv)):
            ref[t] = dot(h, w[...]).astype(BF16).reshape(groups, span, chans)
        c = cot[t].reshape(flat, chans)
        g_s[t] = dot(c, wot[...]).astype(BF16).reshape(groups, span, chans)
        return carry

    lax.fori_loop(0, sources, project, 0)

    place = lax.broadcasted_iota(jnp.int32, (1, chans), 1)
    head_masks = [
        jnp.where((place >= h * HEAD_DIM) & (place < (h + 1) * HEAD_DIM), 1.0, 0.0).astype(BF16)
        for h in range(heads)
    ]
    left = lax.broadcasted_iota(jnp.int32, (size, size), 0)
    right = lax.broadcasted_iota(jnp.int32, (size, size), 1)
    same = (left & (PIXEL_BLOCK - 1)) == (right & (PIXEL_BLOCK - 1))

    def one_group(g, carry):
        def get(ref):
            return ref[:, g].reshape(size, chans)

        def stack(arr):
            return jnp.concatenate([arr * m for m in head_masks], axis=0)

        q, k, v, og = get(q_s), get(k_s), get(v_s), get(g_s)
        kst, vst = stack(k), stack(v)
        scores = dot(q, kst, ((1,), (1,))) * scale
        dprobs = dot(og, vst, ((1,), (1,)))
        lows, lows_t, grads, grads_t = [], [], [], []
        for h in range(heads):
            block = slice(h * size, (h + 1) * size)
            s = jnp.where(same, scores[:, block], -1e30)
            e = jnp.exp(s - jnp.max(s, axis=1, keepdims=True))
            prob = e / jnp.sum(e, axis=1, keepdims=True)
            dp = dprobs[:, block]
            ds = prob * (dp - jnp.sum(prob * dp, axis=1, keepdims=True)) * scale
            low, grad = prob.astype(BF16), ds.astype(BF16)
            lows.append(low)
            grads.append(grad)
            lows_t.append(low.T)
            grads_t.append(grad.T)
        shape = (sources, span, chans)
        low = jnp.concatenate(lows, axis=1)
        grad = jnp.concatenate(grads, axis=1)
        low_t = jnp.concatenate(lows_t, axis=1)
        grad_t = jnp.concatenate(grads_t, axis=1)
        att_o[:, g] = dot(low, vst).astype(BF16).reshape(shape)
        qg_o[:, g] = dot(grad, kst).astype(BF16).reshape(shape)
        kg_o[:, g] = dot(grad_t, stack(q)).astype(BF16).reshape(shape)
        vg_o[:, g] = dot(low_t, stack(og)).astype(BF16).reshape(shape)
        return carry

    lax.fori_loop(0, groups, one_group, 0)

    def back(t, carry):
        total = dot(qg_o[t].reshape(flat, chans), wqt[...])
        total = total + dot(kg_o[t].reshape(flat, chans), wkt[...])
        total = total + dot(vg_o[t].reshape(flat, chans), wvt[...])
        cols_o[t] = total.astype(BF16).reshape(groups, span, chans)
        return carry

    lax.fori_loop(0, sources, back, 0)


def weight_grads_kernel(hid, cot, att, qg, kg, vg, out_ref):
    sources, groups, span, chans = hid.shape
    flat = groups * span
    out_ref[...] = jnp.zeros(out_ref.shape, F32)

    def one(t, carry):
        ht = hid[t].reshape(flat, chans).T
        for i, ref in enumerate((qg, kg, vg)):
            out_ref[i] += dot(ht, ref[t].reshape(flat, chans))
        out_ref[3] += dot(att[t].reshape(flat, chans).T, cot[t].reshape(flat, chans))
        return carry

    lax.fori_loop(0, sources, one, 0)


def hidden_grad_kernel(back_ref, cot_ref, out_ref, first_ref, last_ref):
    frames, rows, cols, chans = cot_ref.shape
    real = rows * cols // PIXEL_BLOCK
    back = back_ref[0:real].astype(F32)
    for f in range(frames):
        piece = back[:, f * PIXEL_BLOCK : (f + 1) * PIXEL_BLOCK].reshape(rows, cols, chans)
        total = (cot_ref[f].astype(F32) + piece).astype(BF16)
        out_ref[f] = total
        first_ref[f] = total[0]
        last_ref[f] = total[rows - 1]


def conv_grad_kernel(top_ref, cells_ref, bottom_ref, grad_ref, out_ref, ext):
    frames, rows, cols, chans = cells_ref.shape
    out_ref[...] = jnp.zeros(out_ref.shape, F32)

    def one_frame(f, carry):
        ext[0] = top_ref[f]
        ext[1 : rows + 1] = cells_ref[f]
        ext[rows + 1] = bottom_ref[f]
        grad = grad_ref[f].reshape(rows * cols, chans)
        wide = grad.astype(F32)
        moved = [
            shifted(wide, 1, rows, cols).astype(BF16),
            grad,
            shifted(wide, -1, rows, cols).astype(BF16),
        ]
        for a in range(3):
            turned = ext[a : a + rows].reshape(rows * cols, chans).T
            for b in range(3):
                at = (3 * a + b) * chans
                out_ref[at : at + chans] += dot(turned, moved[b])
        return carry

    lax.fori_loop(0, frames, one_frame, 0)


def hops(sizes):
    space, tm = sizes
    first = [("space", 1)]
    rest = []
    stride = 2
    while stride < space:
        rest.append(("space", stride))
        stride *= 2
    stride = 1
    while stride < tm:
        rest.append(("tm", stride))
        stride *= 2
    return [first + rest[p:] + rest[:p] for p in range(3)], first + rest


def reduce_kernel(plan, greet, part_rows, x_ref, out_ref, acc, low, send_sems, recv_sems, *recvs):
    def bit_and_partner(axis, stride):
        me = lax.axis_index(axis)
        bit = (me // stride) % 2
        return bit, me + (1 - 2 * bit) * stride

    barrier = pltpu.get_barrier_semaphore()
    for axis, stride in greet:
        _, partner = bit_and_partner(axis, stride)
        pl.semaphore_signal(barrier, inc=1, device_id={axis: partner}, device_id_type=MESH)
    pl.semaphore_wait(barrier, len(greet))

    parts, steps = len(plan), len(plan[0])
    offs = [p * part_rows for p in range(parts)]
    size = part_rows
    for s in range(steps):
        half = size // 2
        src = x_ref if s == 0 else acc
        copies, keeps = [], []
        for p in range(parts):
            axis, stride = plan[p][s]
            bit, partner = bit_and_partner(axis, stride)
            send = pl.multiple_of(offs[p] + (1 - bit) * half, 16)
            keeps.append(pl.multiple_of(offs[p] + bit * half, 16))
            copy = pltpu.make_async_remote_copy(
                src_ref=src.at[pl.ds(send, half)],
                dst_ref=recvs[s].at[p],
                send_sem=send_sems.at[s, p],
                recv_sem=recv_sems.at[s, p],
                device_id={axis: partner},
                device_id_type=MESH,
            )
            copy.start()
            copies.append(copy)
        for p in range(parts):
            copies[p].wait()
            acc[pl.ds(keeps[p], half)] = src[pl.ds(keeps[p], half)] + recvs[s][p]
        offs, size = keeps, half
    for p in range(parts):
        low[pl.ds(offs[p], size)] = acc[pl.ds(offs[p], size)].astype(BF16)
    for s in range(steps - 1, -1, -1):
        copies, wider = [], []
        for p in range(parts):
            axis, stride = plan[p][s]
            bit, partner = bit_and_partner(axis, stride)
            mine = low.at[pl.ds(offs[p], size)]
            copy = pltpu.make_async_remote_copy(
                src_ref=mine,
                dst_ref=mine,
                send_sem=send_sems.at[steps + s, p],
                recv_sem=recv_sems.at[steps + s, p],
                device_id={axis: partner},
                device_id_type=MESH,
            )
            copy.start()
            copies.append(copy)
            wider.append(pl.multiple_of(offs[p] - bit * size, 16))
        for copy in copies:
            copy.wait()
        offs, size = wider, size * 2
    out_ref[...] = low[...].astype(F32)


def total_over_devices(arr, sizes, part_rows):
    plan, greet = hops(sizes)
    steps, parts = len(greet), len(plan)
    chans = arr.shape[1]
    scratch = [
        pltpu.VMEM(arr.shape, F32),
        pltpu.VMEM(arr.shape, BF16),
        pltpu.SemaphoreType.DMA((2 * steps, parts)),
        pltpu.SemaphoreType.DMA((2 * steps, parts)),
    ]
    scratch += [pltpu.VMEM((parts, part_rows >> (s + 1), chans), F32) for s in range(steps)]
    return call(
        functools.partial(reduce_kernel, plan, greet, part_rows),
        shape_of(arr.shape, F32),
        (arr,),
        scratch,
        collective_id=0,
        has_side_effects=True,
    )


def halo(first, last):
    count = lax.axis_size("space")
    up = [(i, i + 1) for i in range(count - 1)]
    down = [(i + 1, i) for i in range(count - 1)]
    return lax.ppermute(last, "space", up), lax.ppermute(first, "space", down)


def on_device(latents, cotangent, conv_weight, query_weight, key_weight, value_weight, out_weight):
    frames, rows, cols, chans = latents.shape
    sizes = (lax.axis_size("space"), lax.axis_size("tm"))
    space, tm = sizes
    whole_count = frames * tm * rows * space * cols
    norm = 1.0 / jnp.sqrt(jnp.float32(whole_count))
    per_source = -(-(rows * cols // PIXEL_BLOCK) // tm)
    groups = per_source * tm
    span = frames * PIXEL_BLOCK
    grouped = (tm, per_source, span, chans)

    def exchange(arr):
        return lax.all_to_all(arr, "tm", split_axis=0, concat_axis=0, tiled=True)

    top, bottom = halo(latents[:, 0], latents[:, rows - 1])
    cot_groups = call(regroup_kernel, shape_of((groups, span, chans), BF16), (cotangent,))
    cot_all = exchange(cot_groups).reshape(grouped)
    weights = conv_weight.reshape(9, chans, chans)
    hidden = convolve(top, latents, bottom, weights, groups)
    hid_all = exchange(hidden).reshape(grouped)
    tile = shape_of(grouped, BF16)
    attn_cols, attended, query_grad, key_grad, value_grad = call(
        attend_kernel,
        (tile,) * 5,
        (
            hid_all,
            cot_all,
            query_weight,
            key_weight,
            value_weight,
            out_weight.T,
            query_weight.T,
            key_weight.T,
            value_weight.T,
        ),
        [pltpu.VMEM(grouped, BF16)] * 4,
        flops=20 * hid_all.size * chans,
    )
    attn_back = exchange(attn_cols.reshape(groups, span, chans))
    small = call(
        weight_grads_kernel,
        shape_of((4, chans, chans), F32),
        (hid_all, cot_all, attended, query_grad, key_grad, value_grad),
        flops=8 * hid_all.size * chans,
    )
    small = lax.psum(small, ("space", "tm")) * norm
    hidden_grad, first, last = call(
        hidden_grad_kernel,
        (
            shape_of(latents.shape, BF16),
            shape_of((frames, cols, chans), BF16),
            shape_of((frames, cols, chans), BF16),
        ),
        (attn_back, cotangent),
    )
    grad_top, grad_bottom = halo(first, last)
    devices = space * tm
    part_rows = -(-9 * chans // (3 * devices * 16)) * devices * 16
    conv_part = call(
        conv_grad_kernel,
        shape_of((3 * part_rows, chans), F32),
        (top, latents, bottom, hidden_grad),
        [pltpu.VMEM((rows + 2, cols, chans), BF16)],
        flops=18 * latents.size * chans,
    )
    turned = jnp.swapaxes(conv_weight[::-1, ::-1], 2, 3).reshape(9, chans, chans)
    grad_input = convolve(grad_top, hidden_grad, grad_bottom, turned)
    conv_total = total_over_devices(conv_part, sizes, part_rows)
    grad_conv = conv_total[: 9 * chans].reshape(3, 3, chans, chans) * norm
    return grad_input, grad_conv, small[0], small[1], small[2], small[3]


def solution(mesh):
    in_specs = (P("tm", "space", None, None), P("tm", "space", None, None), P(), P(), P(), P(), P())
    out_specs = (P("tm", "space", None, None), P(), P(), P(), P(), P())
    return jax.shard_map(
        on_device, mesh=mesh, in_specs=in_specs, out_specs=out_specs, check_vma=False
    )
```

time: 471 us -> 406 us (0.86); the launches traced: 462 us -> 405 us
  Pallas kernels: 0 us -> 138 us
  local copies, waits for them, and re-layouts: 144 us -> 41.1 us
  matrix products: 96.4 us -> 0 us
  waiting for transfers between devices: 163 us -> 183 us
  other arithmetic: 19.8 us -> 6.44 us
    pallas_call x0 -> x8, Pallas kernels: none -> 138 us  [call(): pl.pallas_call(body, out_shape=out_shape, in_specs=[pl.BlockSpec(memory_s...]
    dot_general x43 -> x0, matrix products: 89.4 us -> none  [the longest x25 36.1 us: project(): jnp.dot(arr.reshape(-1, shape[-1]), weight, preferred_element_type=jnp.fl...]
    convert_element_type x11 -> x0, local copies, waits for them, and re-layouts: 56.1 us -> none  [the longest x2 11.6 us: attend(): value_grad = jnp.einsum('whfg,fwhd->gwhd', prob_low, gsplit, preferred_el...]
    reshape x5 -> x0, local copies, waits for them, and re-layouts: 25.4 us -> none  [the longest x4 22.7 us: split(): return arr.reshape(frames, pixels, heads, HEAD_DIM)]
    dot_general x4 -> x0, local copies, waits for them, and re-layouts: 24.6 us -> none  [project(): jnp.dot(arr.reshape(-1, shape[-1]), weight, preferred_element_type=jnp.fl...]
    all_to_all x3, waiting for transfers between devices: 17.6 us -> 41.3 us  [exchange(): return lax.all_to_all(arr, 'tm', split_axis=0, concat_axis=0, tiled=True)]
    another operation x6 -> x0, local copies, waits for them, and re-layouts: 18.7 us -> none  [the longest x5 14.9 us: project(): arr.reshape(-1, shape[-1])]
    unnamed x72 -> x55, local copies, waits for them, and re-layouts: 8.39 us -> 22.7 us
  transfers between devices with their start and end apart: 8 -> 8, of which waited for: 3 -> 4; matrix products, arithmetic and copies ran while one was open for 23% -> 7% of each run, Pallas kernels for 0% -> 24%
where the time goes in v1:
time: 406 us; the launch traced here: 405 us
  waiting for transfers between devices  183 us (45%)
  Pallas kernels  138 us (34%)
  local copies, waits for them, and re-layouts  41.1 us (10%)
  starting transfers between devices  21.7 us (5%)
  between operations  14.3 us (4%)
  other arithmetic  6.44 us (2%)
    psum x1, waiting for transfers between devices, on_device(): small = lax.psum(small, ('space', 'tm')) * norm  141 us
    pallas_call x8, Pallas kernels, call(): pl.pallas_call(body, out_shape=out_shape, in_specs=[pl.BlockSpec(memory_s...  138 us
    all_to_all x3, waiting for transfers between devices, exchange(): return lax.all_to_all(arr, 'tm', split_axis=0, concat_axis=0, tiled=True)  41.3 us
    unnamed x55, local copies, waits for them, and re-layouts  22.7 us
    all_to_all x3, starting transfers between devices, exchange(): return lax.all_to_all(arr, 'tm', split_axis=0, concat_axis=0, tiled=True)  14.5 us
  transfers between devices with their start and end apart: 8, of which 4 were waited for; matrix products, arithmetic and copies ran while one was open for 7% of the time, Pallas kernels for 24%

profile of v1, /device:TPU:0, one launch (start us, length us, event | category | flops | bytes accessed | tf_op | source)
XLA Modules:
  0.0 405.2 jit_solution(4645722990973628530)
XLA Ops:
  7.2 1.8 copy.30.cells_ref.cot_ref
  9.0 0.0 copy-start
  9.0 0.1 shard_map.119
  9.1 0.0 copy-start.5
  9.2 1.3 copy-done.5
  10.4 0.2 copy-done
  10.6 6.3 %all-to-all-start.1 = ((bf16[60,32,320]{2,1,0:T(8,128)(2,1)}), bf16[60,32,320]{2,1,0:T(8,128)(2,1)S(1)}, u32[]{:S(2)}, u32[]{:S(2)}) async-start(bf16[60,32,320]{2,1,0:T(8,128)(2,1)} %copy-done.5), calls=%async_computation.1 | async-start | bytes 2949120 | tf_op jit(solution)/shard_map/all_to_all | solution.py:356
  16.9 2.3 slice_bitcast_fusion
  19.3 2.3 collective-permute-start
  21.6 1.3 collective-permute-start.1
  22.8 0.0 copy-done.23
  22.9 1.5 copy.28.cells_ref
  24.4 0.0 collective-permute-done
  24.4 1.4 copy.27.top_ref
  25.9 0.5 collective-permute-done.1
  26.4 1.4 copy.29.bottom_ref
  27.8 11.3 %shard_map.118 = bf16[60,32,320]{2,1,0:T(8,128)(2,1)S(1)} custom-call(bf16[4,240,320]{2,1,0:T(8,128)(2,1)S(1)} %copy.27.top_ref, bf16[4,2,240,320]{3,2,1,0:T(8,128)(2,1)} %copy.28.cells_ref, bf16[4,240,320]{2,1,0:T(8,128)(2,1)S(1)} %copy.29.bottom_ref, bf16[9,320,320]{2,1,0:T(8,128)(2,1)} %bitcast.38), custom_call_target="tpu_custom_call" | custom-call | flops 3538944000 | bytes 8601600 | tf_op jit(solution)/shard_map/pallas_call | solution.py:20
  39.2 0.0 copy-start.8
  39.2 1.1 copy-done.8
  40.3 11.5 %all-to-all-done.1 = bf16[60,32,320]{2,1,0:T(8,128)(2,1)S(1)} async-done(((bf16[60,32,320]{2,1,0:T(8,128)(2,1)}), bf16[60,32,320]{2,1,0:T(8,128)(2,1)S(1)}, u32[]{:S(2)}, u32[]{:S(2)}) %all-to-all-start.1) | async-done | bytes 1228832 | tf_op jit(solution)/shard_map/all_to_all | solution.py:356
  51.8 3.6 all-to-all-start
  55.4 1.8 copy.31
  57.2 0.0 copy-done.15
  57.2 0.9 copy.32
  58.0 0.9 copy.33
  58.9 0.0 copy-done.1
  58.9 1.8 copy.34
  60.7 29.9 %all-to-all-done = bf16[60,32,320]{2,1,0:T(8,128)(2,1)S(1)} async-done(((bf16[60,32,320]{2,1,0:T(8,128)(2,1)}), bf16[60,32,320]{2,1,0:T(8,128)(2,1)S(1)}, u32[]{:S(2)}, u32[]{:S(2)}) %all-to-all-start) | async-done | bytes 1228832 | tf_op jit(solution)/shard_map/all_to_all | solution.py:356
  90.5 1.1 copy-done.3
  91.6 0.9 copy-done.17
  92.6 0.9 copy-done.18
  93.5 0.9 copy-done.19
  94.5 0.9 copy-done.20
  95.4 0.9 copy-done.21
  96.4 27.3 %shard_map.120 = (bf16[4,15,32,320]{3,2,1,0:T(8,128)(2,1)S(1)}, bf16[4,15,32,320]{3,2,1,0:T(8,128)(2,1)}, bf16[4,15,32,320]{3,2,1,0:T(8,128)(2,1)}, bf16[4,15,32...) custom-call(bf16[4,15,32,320]{3,2,1,0:T(8,128)(2,1)} %bitcast.30, bf16[4,15,32,320]{3,2,1,0:T(8,128)(2,1)} %bitcast.28, ...), custom_call_target="tpu_custom_call" | custom-call | flops 3932160000 | bytes 7782400 | tf_op jit(solution)/shard_map/pallas_call | solution.py:20
  123.7 1.1 copy-done.7
  124.9 4.6 %all-to-all-start.2 = ((bf16[60,32,320]{2,1,0:T(8,128)(2,1)}), bf16[60,32,320]{2,1,0:T(8,128)(2,1)}, u32[]{:S(2)}, u32[]{:S(2)}) async-start(bf16[60,32,320]{2,1,0:T(8,128)(2,1)} %bitcast.32), calls=%async_computation.2 | async-start | bytes 2949120 | tf_op jit(solution)/shard_map/all_to_all | solution.py:356
  129.5 0.0 all-reduce.2.cloned.1.call-start
  129.6 7.7 %shard_map.125 = f32[4,320,320]{2,1,0:T(8,128)} custom-call(bf16[4,15,32,320]{3,2,1,0:T(8,128)(2,1)S(1)} %bitcast.31, bf16[4,15,32,320]{3,2,1,0:T(8,128)(2,1)S(1)} %bitcast.29, bf16[4,15,32,320]{3,2,1,0:T(8,128)(2,1)} %get-tuple-element.18.att, bf16[4,15,32,320]{3,2,1,0:T(8,128)(2,1)} %get-tuple-element.19.qg, ...), custom_call_target="tpu_custom_call" | custom-call | flops 1572864000 | bytes 14745600 | tf_op jit(solution)/shard_map/pallas_call | solution.py:20
  137.2 0.0 all-reduce.2.cloned.1.call-update
  137.2 1.9 reverse_bitcast_fusion
  139.1 2.5 copy.38
  141.6 141.3 %all-reduce.2.cloned.1.call-done = f32[4,320,320]{2,1,0:T(8,128)} async-done(((f32[4,320,320]{2,1,0:T(8,128)}), f32[4,320,320]{2,1,0:T(8,128)}) %all-reduce.2.cloned.1.call-update) | async-done | bytes 1638416 | tf_op jit(solution)/shard_map/psum | solution.py:389
  282.9 1.7 broadcast_multiply_fusion
  284.6 1.3 slice_bitcast_fusion.2
  285.9 0.0 all-to-all-done.2.back_ref
  285.9 2.2 shard_map.121
  288.2 0.0 copy-start.13
  288.2 0.9 copy-done.13
  289.1 0.9 copy-done.14
  289.9 1.2 copy-done.22
  291.1 2.4 copy.36
  293.5 2.1 collective-permute-start.2
  295.6 2.2 copy.37
  297.9 1.5 collective-permute-start.3
  299.4 10.9 %shard_map.123.x_ref = f32[3072,320]{1,0:T(8,128)} custom-call(bf16[4,240,320]{2,1,0:T(8,128)(2,1)S(1)} %copy-done.10, bf16[4,2,240,320]{3,2,1,0:T(8,128)(2,1)S(1)} %copy-done.6, bf16[4,240,320]{2,1,0:T(8,128)(2,1)S(1)} %copy-done.12, bf16[4,2,240,320]{3,2,1,0:T(8,128)(2,1)} %copy-done.22), custom_call_target="tpu_custom_call" | custom-call | flops 3538944000 | bytes 7372800 | tf_op jit(solution)/shard_map/pallas_call | solution.py:20
  310.3 67.9 %shard_map.124 = f32[3072,320]{1,0:T(8,128)} custom-call(f32[3072,320]{1,0:T(8,128)} %shard_map.123.x_ref), custom_call_target="tpu_custom_call" | custom-call | bytes 7864320 | tf_op jit(solution)/shard_map/pallas_call | solution.py:20
  378.2 4.7 %slice_multiply_fusion = f32[2880,320]{1,0:T(8,128)} fusion(f32[3072,320]{1,0:T(8,128)} %shard_map.124), kind=kLoop, calls=%fused_computation | loop fusion | flops 921600 | bytes 7372800 | tf_op jit(solution)/shard_map/mul | solution.py:412
  382.9 0.0 collective-permute-done.2
  382.9 1.4 copy.39.top_ref
  384.4 0.0 collective-permute-done.3
  384.4 1.4 copy.40.bottom_ref
  385.8 11.0 %shard_map.122 = bf16[4,2,240,320]{3,2,1,0:T(8,128)(2,1)S(1)} custom-call(bf16[4,240,320]{2,1,0:T(8,128)(2,1)S(1)} %copy.39.top_ref, bf16[4,2,240,320]{3,2,1,0:T(8,128)(2,1)} %copy-done.22, bf16[4,240,320]{2,1,0:T(8,128)(2,1)S(1)} %copy.40.bottom_ref, bf16[9,320,320]{2,1,0:T(8,128)(2,1)} %bitcast.39), custom_call_target="tpu_custom_call" | custom-call | flops 3538944000 | bytes 8601600 | tf_op jit(solution)/shard_map/pallas_call | solution.py:20
  396.8 1.6 copy.44
  (28 shorter events, 0.0 us)
Async XLA Ops:
  9.0 1.6 copy-start
  9.1 1.3 copy-start.5
  10.6 41.2 %all-to-all-start.1 = ((bf16[60,32,320]{2,1,0:T(8,128)(2,1)}), bf16[60,32,320]{2,1,0:T(8,128)(2,1)S(1)}, u32[]{:S(2)}, u32[]{:S(2)}) async-start(bf16[60,32,320]{2,1,0:T(8,128)(2,1)} %copy-done.5), calls=%async_computation.1 | async-start | bytes 2949120 | tf_op jit(solution)/shard_map/all_to_all | solution.py:356
  16.9 5.9 %copy-start.23 = (bf16[4,2,240,320]{2,3,1,0:T(8,128)(2,1)S(1)}, bf16[4,2,240,320]{2,3,1,0:T(8,128)(2,1)}, u32[]{:S(2)}) copy-start(bf16[4,2,240,320]{2,3,1,0:T(8,128)(2,1)} %param.7) | copy-start | bytes 3686404
  19.3 5.1 %collective-permute-start = (bf16[4,240,320]{1,2,0:T(8,128)(2,1)}, bf16[4,240,320]{1,2,0:T(8,128)(2,1)}, u32[]{:S(2)}, u32[]{:S(2)}) collective-permute-start(bf16[4,240,320]{1,2,0:T(8,128)(2,1)} %get-tuple-element.39), channel_id=1, source_target_pairs={{0,4},{4,8},{8,12},{12,16},{16,20},{20,24},{24,28},{1,5},{5,9},{9,... | collective-permute-start | bytes 1843208 | tf_op jit(solution)/shard_map/ppermute | solution.py:341
  21.6 4.8 %collective-permute-start.1 = (bf16[4,240,320]{1,2,0:T(8,128)(2,1)S(1)}, bf16[4,240,320]{1,2,0:T(8,128)(2,1)}, u32[]{:S(2)}, u32[]{:S(2)}) collective-permute-start(bf16[4,240,320]{1,2,0:T(8,128)(2,1)S(1)} %get-tuple-element.38), channel_id=1, source_target_pairs={{4,0},{8,4},{12,8},{16,12},{20,16},{24,20},{28,24},{5,1},{9,5},{13... | collective-permute-start | bytes 1843208 | tf_op jit(solution)/shard_map/ppermute | solution.py:341
  25.8 13.3 %copy-start.9 = (bf16[4,240,320]{2,1,0:T(8,128)(2,1)}, bf16[4,240,320]{2,1,0:T(8,128)(2,1)S(1)}, u32[]{:S(2)}) copy-start(bf16[4,240,320]{2,1,0:T(8,128)(2,1)S(1)} %copy.27.top_ref) | copy-start | bytes 1843204
  27.8 11.4 %copy-start.11 = (bf16[4,240,320]{2,1,0:T(8,128)(2,1)}, bf16[4,240,320]{2,1,0:T(8,128)(2,1)S(1)}, u32[]{:S(2)}) copy-start(bf16[4,240,320]{2,1,0:T(8,128)(2,1)S(1)} %copy.29.bottom_ref) | copy-start | bytes 1843204
  39.2 1.1 copy-start.8
  40.3 16.8 %copy-start.15 = (bf16[320,320]{1,0:T(8,128)(2,1)S(1)}, bf16[320,320]{1,0:T(8,128)(2,1)}, u32[]{:S(2)}) copy-start(bf16[320,320]{1,0:T(8,128)(2,1)} %wq.1) | copy-start | bytes 614404
  40.3 17.7 %copy-start.16 = (bf16[320,320]{1,0:T(8,128)(2,1)S(1)}, bf16[320,320]{1,0:T(8,128)(2,1)}, u32[]{:S(2)}) copy-start(bf16[320,320]{1,0:T(8,128)(2,1)} %wk.1) | copy-start | bytes 614404
  51.8 7.1 %copy-start.1 = (bf16[60,32,320]{2,1,0:T(8,128)(2,1)}, bf16[60,32,320]{2,1,0:T(8,128)(2,1)S(1)}, u32[]{:S(2)}) copy-start(bf16[60,32,320]{2,1,0:T(8,128)(2,1)S(1)} %all-to-all-done.1) | copy-start | bytes 3686404
  51.8 38.7 %all-to-all-start = ((bf16[60,32,320]{2,1,0:T(8,128)(2,1)}), bf16[60,32,320]{2,1,0:T(8,128)(2,1)S(1)}, u32[]{:S(2)}, u32[]{:S(2)}) async-start(bf16[60,32,320]{2,1,0:T(8,128)(2,1)} %copy-done.8), calls=%async_computation | async-start | bytes 2949120 | tf_op jit(solution)/shard_map/all_to_all | solution.py:356
  90.5 1.1 copy-start.3
  91.6 0.9 copy-start.17
  92.6 0.9 copy-start.18
  93.5 0.9 copy-start.19
  94.5 0.9 copy-start.20
  95.4 0.9 copy-start.21
  123.7 1.1 copy-start.7
  124.8 4.7 %copy-start.2 = (bf16[60,32,320]{2,1,0:T(8,128)(2,1)S(1)}, bf16[60,32,320]{2,1,0:T(8,128)(2,1)}, u32[]{:S(2)}) copy-start(bf16[60,32,320]{2,1,0:T(8,128)(2,1)} %copy-done.1) | copy-start | bytes 3686404
  124.9 4.7 %copy-start.4 = (bf16[60,32,320]{2,1,0:T(8,128)(2,1)S(1)}, bf16[60,32,320]{2,1,0:T(8,128)(2,1)}, u32[]{:S(2)}) copy-start(bf16[60,32,320]{2,1,0:T(8,128)(2,1)} %copy-done.3) | copy-start | bytes 3686404
  124.9 161.1 %all-to-all-start.2 = ((bf16[60,32,320]{2,1,0:T(8,128)(2,1)}), bf16[60,32,320]{2,1,0:T(8,128)(2,1)}, u32[]{:S(2)}, u32[]{:S(2)}) async-start(bf16[60,32,320]{2,1,0:T(8,128)(2,1)} %bitcast.32), calls=%async_computation.2 | async-start | bytes 2949120 | tf_op jit(solution)/shard_map/all_to_all | solution.py:356
  129.5 153.4 %all-reduce.2.cloned.1.call-start = ((), (), s32[]{:S(2)}) async-start(), calls=%async_computation.3 | async-start | bytes 3932160 | tf_op jit(solution)/shard_map/psum | solution.py:389
  285.9 13.4 %copy-start.12 = (bf16[4,240,320]{2,1,0:T(8,128)(2,1)S(1)}, bf16[4,240,320]{2,1,0:T(8,128)(2,1)}, u32[]{:S(2)}) copy-start(bf16[4,240,320]{2,1,0:T(8,128)(2,1)} %copy-done.11) | copy-start | bytes 1843204
  288.2 0.9 copy-start.13
  289.1 0.9 copy-start.14
  289.9 1.2 copy-start.22
  291.1 8.2 %copy-start.6 = (bf16[4,2,240,320]{3,2,1,0:T(8,128)(2,1)S(1)}, bf16[4,2,240,320]{3,2,1,0:T(8,128)(2,1)}, u32[]{:S(2)}) copy-start(bf16[4,2,240,320]{3,2,1,0:T(8,128)(2,1)} %copy.28.cells_ref) | copy-start | bytes 3686404
  291.1 8.3 %copy-start.10 = (bf16[4,240,320]{2,1,0:T(8,128)(2,1)S(1)}, bf16[4,240,320]{2,1,0:T(8,128)(2,1)}, u32[]{:S(2)}) copy-start(bf16[4,240,320]{2,1,0:T(8,128)(2,1)} %copy-done.9) | copy-start | bytes 1843204
  293.5 89.4 %collective-permute-start.2 = (bf16[4,240,320]{1,2,0:T(8,128)(2,1)}, bf16[4,240,320]{1,2,0:T(8,128)(2,1)}, u32[]{:S(2)}, u32[]{:S(2)}) collective-permute-start(bf16[4,240,320]{1,2,0:T(8,128)(2,1)} %copy.36), channel_id=1, source_target_pairs={{0,4},{4,8},{8,12},{12,16},{16,20},{20,24},{24,28},{1,5},{5,9},{9,... | collective-permute-start | bytes 1843208 | tf_op jit(solution)/shard_map/ppermute | solution.py:341
  297.9 86.5 %collective-permute-start.3 = (bf16[4,240,320]{1,2,0:T(8,128)(2,1)}, bf16[4,240,320]{1,2,0:T(8,128)(2,1)}, u32[]{:S(2)}, u32[]{:S(2)}) collective-permute-start(bf16[4,240,320]{1,2,0:T(8,128)(2,1)} %copy.37), channel_id=1, source_target_pairs={{4,0},{8,4},{12,8},{16,12},{20,16},{24,20},{28,24},{5,1},{9,5},{13... | collective-permute-start | bytes 1843208 | tf_op jit(solution)/shard_map/ppermute | solution.py:341
Sparse Core Ops, SparseCore 0:
  137.4 145.5 all-reduce.1

commit v2 on v1

--- a/solution.py
+++ b/solution.py
@@ -9,6 +9,7 @@
 
 HEAD_DIM = 64
 PIXEL_BLOCK = 8
+LANES = 128
 F32 = jnp.float32
 BF16 = jnp.bfloat16
 VMEM_BYTES = 50 * 1024 * 1024
@@ -36,15 +37,32 @@
     return lax.dot_general(left, right, (dims, ((), ())), preferred_element_type=F32)
 
 
-def shifted(arr, step, rows, cols):
-    total = rows * cols
-    moved = pltpu.roll(arr, (-step) % total, 0)
-    place = lax.broadcasted_iota(jnp.int32, arr.shape, 0)
-    edge = None
-    for row in range(rows):
-        hit = place == (row * cols + (0 if step < 0 else cols - 1))
-        edge = hit if edge is None else edge | hit
-    return jnp.where(edge, 0.0, moved)
+def shifted(arr, step, rows, cols, pad):
+    chans = arr.shape[-1]
+    edge = 7 if step < 0 else cols + 8
+    pad[:, edge : edge + 1] = jnp.zeros((rows, 1, chans), F32)
+    pad[:, 8 : cols + 8] = arr.reshape(rows, cols, chans)
+    return pad[:, 8 + step : 8 + step + cols].reshape(rows * cols, chans)
+
+
+def conv_frame(f, top_ref, cells_ref, bottom_ref, weight_ref, ext, pad):
+    frames, rows, cols, chans = cells_ref.shape
+    ext[0] = top_ref[f]
+    ext[1 : rows + 1] = cells_ref[f]
+    ext[rows + 1] = bottom_ref[f]
+    total = cells_ref[f].reshape(rows * cols, chans).astype(F32)
+    for b in range(3):
+        part = None
+        for a in range(3):
+            piece = ext[a : a + rows].reshape(rows * cols, chans)
+            prod = dot(piece, weight_ref[3 * a + b])
+            part = prod if part is None else part + prod
+        total = total + (part if b == 1 else shifted(part, b - 1, rows, cols, pad))
+    return total
+
+
+def conv_scratch(rows, cols, chans):
+    return [pltpu.VMEM((rows + 2, cols, chans), BF16), pltpu.VMEM((rows, cols + 16, chans), F32)]
 
 
 def regroup(parts, groups):
@@ -62,48 +80,27 @@
         out_ref[real:] = jnp.zeros((out_ref.shape[0] - real,) + out_ref.shape[1:], BF16)
 
 
-def conv_kernel(grouped, top_ref, cells_ref, bottom_ref, weight_ref, out_ref, ext, *scratch):
+def conv_kernel(top_ref, cells_ref, bottom_ref, weight_ref, out_ref, ext, pad, held):
     frames, rows, cols, chans = cells_ref.shape
 
     def one_frame(f, carry):
-        ext[0] = top_ref[f]
-        ext[1 : rows + 1] = cells_ref[f]
-        ext[rows + 1] = bottom_ref[f]
-        total = cells_ref[f].reshape(rows * cols, chans).astype(F32)
-        for b in range(3):
-            part = None
-            for a in range(3):
-                piece = ext[a : a + rows].reshape(rows * cols, chans)
-                prod = dot(piece, weight_ref[3 * a + b])
-                part = prod if part is None else part + prod
-            total = total + (part if b == 1 else shifted(part, b - 1, rows, cols))
-        if grouped:
-            scratch[0][f] = total
-        else:
-            out_ref[f] = total.astype(BF16).reshape(rows, cols, chans)
+        held[f] = conv_frame(f, top_ref, cells_ref, bottom_ref, weight_ref, ext, pad)
         return carry
 
     lax.fori_loop(0, frames, one_frame, 0)
-    if grouped:
-        real = rows * cols // PIXEL_BLOCK
-        out_ref[0:real] = regroup([scratch[0][f] for f in range(frames)], real)
-        if out_ref.shape[0] > real:
-            out_ref[real:] = jnp.zeros((out_ref.shape[0] - real,) + out_ref.shape[1:], BF16)
-
-
-def convolve(top, cells, bottom, weight, groups=None):
+    real = rows * cols // PIXEL_BLOCK
+    out_ref[0:real] = regroup([held[f] for f in range(frames)], real)
+    if out_ref.shape[0] > real:
+        out_ref[real:] = jnp.zeros((out_ref.shape[0] - real,) + out_ref.shape[1:], BF16)
+
+
+def convolve(top, cells, bottom, weight, groups):
     frames, rows, cols, chans = cells.shape
-    scratch = [pltpu.VMEM((rows + 2, cols, chans), BF16)]
-    if groups is None:
-        out = shape_of(cells.shape, BF16)
-    else:
-        out = shape_of((groups, frames * PIXEL_BLOCK, chans), BF16)
-        scratch.append(pltpu.VMEM((frames, rows * cols, chans), F32))
     return call(
-        functools.partial(conv_kernel, groups is not None),
-        out,
+        conv_kernel,
+        shape_of((groups, frames * PIXEL_BLOCK, chans), BF16),
         (top, cells, bottom, weight),
-        scratch,
+        conv_scratch(rows, cols, chans) + [pltpu.VMEM((frames, rows * cols, chans), F32)],
         flops=18 * cells.size * chans,
     )
 
@@ -183,19 +180,51 @@
     lax.fori_loop(0, sources, back, 0)
 
 
-def weight_grads_kernel(hid, cot, att, qg, kg, vg, out_ref):
+def pack_places(count, chans):
+    whole, rest = chans // LANES, chans % LANES
+    places, row = [], 0
+    for m in range(count):
+        for block in range(whole):
+            places.append((row, 0, m, block * LANES, LANES))
+            row += chans
+    lane = 0
+    for m in range(count if rest else 0):
+        places.append((row, lane, m, whole * LANES, rest))
+        lane += rest
+        if lane + rest > LANES:
+            row, lane = row + chans, 0
+    return places, row + (chans if lane else 0)
+
+
+def pack(total, out_ref):
+    count, chans, _ = total.shape
+    places, used = pack_places(count, chans)
+    out_ref[used:] = jnp.zeros((out_ref.shape[0] - used, LANES), F32)
+    if places[-1][1] + places[-1][4] < LANES:
+        out_ref[used - chans : used] = jnp.zeros((chans, LANES), F32)
+    for row, lane, m, col, width in places:
+        out_ref[row : row + chans, lane : lane + width] = total[m, :, col : col + width]
+
+
+def part_size(count, chans, parts, devices):
+    unit = parts * devices * 16
+    return -(-pack_places(count, chans)[1] // unit) * devices * 16
+
+
+def weight_grads_kernel(hid, cot, att, qg, kg, vg, out_ref, total):
     sources, groups, span, chans = hid.shape
     flat = groups * span
-    out_ref[...] = jnp.zeros(out_ref.shape, F32)
+    total[...] = jnp.zeros(total.shape, F32)
 
     def one(t, carry):
         ht = hid[t].reshape(flat, chans).T
         for i, ref in enumerate((qg, kg, vg)):
-            out_ref[i] += dot(ht, ref[t].reshape(flat, chans))
-        out_ref[3] += dot(att[t].reshape(flat, chans).T, cot[t].reshape(flat, chans))
+            total[i] += dot(ht, ref[t].reshape(flat, chans))
+        total[3] += dot(att[t].reshape(flat, chans).T, cot[t].reshape(flat, chans))
         return carry
 
     lax.fori_loop(0, sources, one, 0)
+    pack(total, out_ref)
 
 
 def hidden_grad_kernel(back_ref, cot_ref, out_ref, first_ref, last_ref):
@@ -210,9 +239,9 @@
         last_ref[f] = total[rows - 1]
 
 
-def conv_grad_kernel(top_ref, cells_ref, bottom_ref, grad_ref, out_ref, ext):
+def conv_grad_kernel(top_ref, cells_ref, bottom_ref, grad_ref, out_ref, ext, pad, total):
     frames, rows, cols, chans = cells_ref.shape
-    out_ref[...] = jnp.zeros(out_ref.shape, F32)
+    total[...] = jnp.zeros(total.shape, F32)
 
     def one_frame(f, carry):
         ext[0] = top_ref[f]
@@ -221,36 +250,46 @@
         grad = grad_ref[f].reshape(rows * cols, chans)
         wide = grad.astype(F32)
         moved = [
-            shifted(wide, 1, rows, cols).astype(BF16),
+            shifted(wide, 1, rows, cols, pad).astype(BF16),
             grad,
-            shifted(wide, -1, rows, cols).astype(BF16),
+            shifted(wide, -1, rows, cols, pad).astype(BF16),
         ]
         for a in range(3):
             turned = ext[a : a + rows].reshape(rows * cols, chans).T
             for b in range(3):
-                at = (3 * a + b) * chans
-                out_ref[at : at + chans] += dot(turned, moved[b])
+                total[3 * a + b] += dot(turned, moved[b])
         return carry
 
     lax.fori_loop(0, frames, one_frame, 0)
-
-
-def hops(sizes):
+    pack(total, out_ref)
+
+
+def hops(sizes, parts, links_first):
     space, tm = sizes
-    first = [("space", 1)]
-    rest = []
+    first, planes, line = [("space", 1)], [], []
     stride = 2
     while stride < space:
-        rest.append(("space", stride))
+        planes.append(("space", stride))
         stride *= 2
     stride = 1
     while stride < tm:
-        rest.append(("tm", stride))
+        line.append(("tm", stride))
         stride *= 2
-    return [first + rest[p:] + rest[:p] for p in range(3)], first + rest
-
-
-def reduce_kernel(plan, greet, part_rows, x_ref, out_ref, acc, low, send_sems, recv_sems, *recvs):
+    if links_first:
+        plan = [first + planes[p:] + planes[:p] + line for p in range(parts)]
+    else:
+        rest = planes + line
+        plan = [first + rest[p:] + rest[:p] for p in range(parts)]
+    return plan, first + planes + line
+
+
+def reduce_kernel(plan, greet, part_rows, norm, beside, *refs):
+    if beside:
+        x_ref, top_ref, cells_ref, bottom_ref, weight_ref, out_ref, result_ref = refs[:7]
+        ext, pad, acc, low, send_sems, recv_sems, *recvs = refs[7:]
+    else:
+        x_ref, out_ref, acc, low, send_sems, recv_sems, *recvs = refs
+
     def bit_and_partner(axis, stride):
         me = lax.axis_index(axis)
         bit = (me // stride) % 2
@@ -284,6 +323,11 @@
             )
             copy.start()
             copies.append(copy)
+        if beside:
+            frames, rows, cols, chans = cells_ref.shape
+            for f in range(s, frames, steps):
+                total = conv_frame(f, top_ref, cells_ref, bottom_ref, weight_ref, ext, pad)
+                result_ref[f] = total.astype(BF16).reshape(rows, cols, chans)
         for p in range(parts):
             copies[p].wait()
             acc[pl.ds(keeps[p], half)] = src[pl.ds(keeps[p], half)] + recvs[s][p]
@@ -310,26 +354,33 @@
         for copy in copies:
             copy.wait()
         offs, size = wider, size * 2
-    out_ref[...] = low[...].astype(F32)
-
-
-def total_over_devices(arr, sizes, part_rows):
-    plan, greet = hops(sizes)
-    steps, parts = len(greet), len(plan)
-    chans = arr.shape[1]
-    scratch = [
+    count, chans, _ = out_ref.shape
+    for row, lane, m, col, width in pack_places(count, chans)[0]:
+        piece = low[row : row + chans, lane : lane + width].astype(F32)
+        out_ref[m, :, col : col + width] = piece * norm
+
+
+def total_over_devices(arr, count, chans, norm, sizes, parts, part_rows, links_first, number, conv=()):
+    plan, greet = hops(sizes, parts, links_first)
+    steps = len(greet)
+    out = shape_of((count, chans, chans), F32)
+    scratch = []
+    if conv:
+        out = (out, shape_of(conv[1].shape, BF16))
+        scratch += conv_scratch(*conv[1].shape[1:])
+    scratch += [
         pltpu.VMEM(arr.shape, F32),
         pltpu.VMEM(arr.shape, BF16),
         pltpu.SemaphoreType.DMA((2 * steps, parts)),
         pltpu.SemaphoreType.DMA((2 * steps, parts)),
     ]
-    scratch += [pltpu.VMEM((parts, part_rows >> (s + 1), chans), F32) for s in range(steps)]
+    scratch += [pltpu.VMEM((parts, part_rows >> (s + 1), LANES), F32) for s in range(steps)]
     return call(
-        functools.partial(reduce_kernel, plan, greet, part_rows),
-        shape_of(arr.shape, F32),
-        (arr,),
+        functools.partial(reduce_kernel, plan, greet, part_rows, norm, bool(conv)),
+        out,
+        (arr,) + conv,
         scratch,
-        collective_id=0,
+        collective_id=number,
         has_side_effects=True,
     )
 
@@ -346,7 +397,8 @@
     sizes = (lax.axis_size("space"), lax.axis_size("tm"))
     space, tm = sizes
     whole_count = frames * tm * rows * space * cols
-    norm = 1.0 / jnp.sqrt(jnp.float32(whole_count))
+    norm = float(whole_count) ** -0.5
+    devices = space * tm
     per_source = -(-(rows * cols // PIXEL_BLOCK) // tm)
     groups = per_source * tm
     span = frames * PIXEL_BLOCK
@@ -380,13 +432,16 @@
         flops=20 * hid_all.size * chans,
     )
     attn_back = exchange(attn_cols.reshape(groups, span, chans))
+    small_rows = part_size(4, chans, 2, devices)
     small = call(
         weight_grads_kernel,
-        shape_of((4, chans, chans), F32),
+        shape_of((2 * small_rows, LANES), F32),
         (hid_all, cot_all, attended, query_grad, key_grad, value_grad),
+        [pltpu.VMEM((4, chans, chans), F32)],
         flops=8 * hid_all.size * chans,
     )
-    small = lax.psum(small, ("space", "tm")) * norm
+    small = total_over_devices(small, 4, chans, norm, sizes, 2, small_rows, True, 0)
+    attn_back, small = lax.optimization_barrier((attn_back, small))
     hidden_grad, first, last = call(
         hidden_grad_kernel,
         (
@@ -397,19 +452,28 @@
         (attn_back, cotangent),
     )
     grad_top, grad_bottom = halo(first, last)
-    devices = space * tm
-    part_rows = -(-9 * chans // (3 * devices * 16)) * devices * 16
+    part_rows = part_size(9, chans, 3, devices)
     conv_part = call(
         conv_grad_kernel,
-        shape_of((3 * part_rows, chans), F32),
+        shape_of((3 * part_rows, LANES), F32),
         (top, latents, bottom, hidden_grad),
-        [pltpu.VMEM((rows + 2, cols, chans), BF16)],
+        conv_scratch(rows, cols, chans) + [pltpu.VMEM((9, chans, chans), F32)],
         flops=18 * latents.size * chans,
     )
     turned = jnp.swapaxes(conv_weight[::-1, ::-1], 2, 3).reshape(9, chans, chans)
-    grad_input = convolve(grad_top, hidden_grad, grad_bottom, turned)
-    conv_total = total_over_devices(conv_part, sizes, part_rows)
-    grad_conv = conv_total[: 9 * chans].reshape(3, 3, chans, chans) * norm
+    grad_conv, grad_input = total_over_devices(
+        conv_part,
+        9,
+        chans,
+        norm,
+        sizes,
+        3,
+        part_rows,
+        False,
+        1,
+        (grad_top, hidden_grad, grad_bottom, turned),
+    )
+    grad_conv = grad_conv.reshape(3, 3, chans, chans)
     return grad_input, grad_conv, small[0], small[1], small[2], small[3]
 
 

time: 406 us -> 271 us (0.67)
  waiting for transfers between devices: 183 us -> 46.9 us
  Pallas kernels: 138 us -> 168 us
  between operations: 14.3 us -> 0.87 us
  local copies, waits for them, and re-layouts: 41.1 us -> 32.9 us
  other arithmetic: 6.44 us -> 0 us
    psum x1 -> x0, waiting for transfers between devices: 141 us -> none  [on_device(): small = lax.psum(small, ('space', 'tm')) * norm]
    pallas_call x8, Pallas kernels: 138 us -> 168 us  [call(): pl.pallas_call(body, out_shape=out_shape, in_specs=[pl.BlockSpec(memory_s...]
    mul x2 -> x0, other arithmetic: 6.44 us -> none  [the longest x1 4.72 us: on_device(): grad_conv = conv_total[:9 * chans].reshape(3, 3, chans, chans) * norm]
    all_to_all x3, waiting for transfers between devices: 41.3 us -> 46.4 us  [exchange(): return lax.all_to_all(arr, 'tm', split_axis=0, concat_axis=0, tiled=True)]
    unnamed x55 -> x44, local copies, waits for them, and re-layouts: 22.7 us -> 17.8 us
  transfers between devices with their start and end apart: 8 -> 7, of which waited for: 4 -> 3; matrix products, arithmetic and copies ran while one was open for 7% -> 6% of each run, Pallas kernels for 24% -> 27%
where the time goes in v2:
time: 271 us; the launch traced here: 270 us
  Pallas kernels  168 us (62%)
  waiting for transfers between devices  46.9 us (17%)
  local copies, waits for them, and re-layouts  32.9 us (12%)
  starting transfers between devices  22.1 us (8%)
    pallas_call x8, Pallas kernels, call(): pl.pallas_call(body, out_shape=out_shape, in_specs=[pl.BlockSpec(memory_s...  168 us
    all_to_all x3, waiting for transfers between devices, exchange(): return lax.all_to_all(arr, 'tm', split_axis=0, concat_axis=0, tiled=True)  46.4 us
    unnamed x44, local copies, waits for them, and re-layouts  17.8 us
    all_to_all x3, starting transfers between devices, exchange(): return lax.all_to_all(arr, 'tm', split_axis=0, concat_axis=0, tiled=True)  14.5 us
    ppermute x4, starting transfers between devices, halo(): return (lax.ppermute(last, 'space', up), lax.ppermute(first, 'space', down))  7.61 us
    transpose x2, local copies, waits for them, and re-layouts, on_device(): jnp.swapaxes(conv_weight[::-1, ::-1], 2, 3).reshape(9, chans, chans)  5.95 us
  transfers between devices with their start and end apart: 7, of which 3 were waited for; matrix products, arithmetic and copies ran while one was open for 6% of the time, Pallas kernels for 27%

profile of v2, /device:TPU:0, one launch (start us, length us, event | category | flops | bytes accessed | tf_op | source)
XLA Modules:
  0.0 270.5 jit_solution(14958526768183243322)
XLA Ops:
  0.6 1.8 copy.30.cells_ref.cot_ref
  2.5 0.0 copy-start
  2.5 1.4 shard_map.119
  3.9 0.2 copy-done
  4.1 6.4 %all-to-all-start.1 = ((bf16[60,32,320]{2,1,0:T(8,128)(2,1)}), bf16[60,32,320]{2,1,0:T(8,128)(2,1)S(1)}, u32[]{:S(2)}, u32[]{:S(2)}) async-start(bf16[60,32,320]{2,1,0:T(8,128)(2,1)} %shard_map.119), calls=%async_computation.1 | async-start | bytes 2949120 | tf_op jit(solution)/shard_map/all_to_all | solution.py:408
  10.5 0.0 copy-done.16
  10.5 0.9 slice_bitcast_fusion
  11.4 2.3 collective-permute-start
  13.7 1.3 collective-permute-start.1
  15.0 1.6 copy.37.cells_ref
  16.6 0.0 collective-permute-done
  16.6 1.4 copy.36.top_ref
  18.1 0.0 copy-start.9
  18.1 0.5 collective-permute-done.1
  18.6 1.4 copy.38.bottom_ref
  20.0 0.0 copy-start.11
  20.0 11.6 %shard_map.118 = bf16[60,32,320]{2,1,0:T(8,128)(2,1)S(1)} custom-call(bf16[4,240,320]{2,1,0:T(8,128)(2,1)S(1)} %copy.36.top_ref, bf16[4,2,240,320]{3,2,1,0:T(8,128)(2,1)} %copy.37.cells_ref, bf16[4,240,320]{2,1,0:T(8,128)(2,1)S(1)} %copy.38.bottom_ref, bf16[9,320,320]{2,1,0:T(8,128)(2,1)} %bitcast.38), custom_call_target="tpu_custom_call" | custom-call | flops 3538944000 | bytes 8601600 | tf_op jit(solution)/shard_map/pallas_call | solution.py:21
  31.7 0.0 copy-done.9
  31.7 0.0 copy-done.11
  31.7 0.0 copy-start.8
  31.7 1.1 copy-done.8
  32.8 12.6 %all-to-all-done.1 = bf16[60,32,320]{2,1,0:T(8,128)(2,1)S(1)} async-done(((bf16[60,32,320]{2,1,0:T(8,128)(2,1)}), bf16[60,32,320]{2,1,0:T(8,128)(2,1)S(1)}, u32[]{:S(2)}, u32[]{:S(2)}) %all-to-all-start.1) | async-done | bytes 1228832 | tf_op jit(solution)/shard_map/all_to_all | solution.py:408
  45.4 1.2 copy-done.2
  46.5 3.6 %all-to-all-start = ((bf16[60,32,320]{2,1,0:T(8,128)(2,1)}), bf16[60,32,320]{2,1,0:T(8,128)(2,1)S(1)}, u32[]{:S(2)}, u32[]{:S(2)}) async-start(bf16[60,32,320]{2,1,0:T(8,128)(2,1)} %copy-done.8), calls=%async_computation | async-start | bytes 2949120 | tf_op jit(solution)/shard_map/all_to_all | solution.py:408
  50.1 0.0 copy-start.15
  50.1 1.2 copy.31
  51.3 0.0 copy-done.13
  51.3 0.2 copy.32
  51.5 0.0 copy-done.14
  51.5 0.2 copy.33
  51.7 0.0 copy-done.15
  51.7 0.2 copy.34
  51.9 33.9 %all-to-all-done = bf16[60,32,320]{2,1,0:T(8,128)(2,1)S(1)} async-done(((bf16[60,32,320]{2,1,0:T(8,128)(2,1)}), bf16[60,32,320]{2,1,0:T(8,128)(2,1)S(1)}, u32[]{:S(2)}, u32[]{:S(2)}) %all-to-all-start) | async-done | bytes 1228832 | tf_op jit(solution)/shard_map/all_to_all | solution.py:408
  85.8 1.2 copy-done.4
  86.9 28.2 %shard_map.120 = (bf16[4,15,32,320]{3,2,1,0:T(8,128)(2,1)}, bf16[4,15,32,320]{3,2,1,0:T(8,128)(2,1)}, bf16[4,15,32,320]{3,2,1,0:T(8,128)(2,1)}, bf16[4,15,32,320]{3,2,1,0:T(8,128)(2,1)}, bf16[4,15,32,320]{3,2,1,0:T(8,128)(2,1)}) custom-call(bf16[4,15,32,320]{3,2,1,0:T(8,128)(2,1)} %bitcast.30, bf16[4,15,32,320]{3,2,1,0:T(8,128)(2,1)} %bitcast.28, ...), custom_call_target="tpu_custom_call" | custom-call | flops 3932160000 | bytes 7782400 | tf_op jit(solution)/shard_map/pallas_call | solution.py:21
  115.1 4.5 %all-to-all-start.2 = ((bf16[60,32,320]{2,1,0:T(8,128)(2,1)}), bf16[60,32,320]{2,1,0:T(8,128)(2,1)}, u32[]{:S(2)}, u32[]{:S(2)}) async-start(bf16[60,32,320]{2,1,0:T(8,128)(2,1)} %bitcast.9), calls=%async_computation.2 | async-start | bytes 2949120 | tf_op jit(solution)/shard_map/all_to_all | solution.py:408
  119.6 0.0 copy-done.17
  119.6 1.6 reverse_bitcast_fusion
  121.2 4.3 %copy.41 = bf16[3,3,320,320]{3,2,1,0:T(8,128)(2,1)} copy(bf16[3,3,320,320]{2,3,1,0:T(8,128)(2,1)} %reverse_bitcast_fusion) | data formatting | bytes 3686400 | tf_op jit(solution)/shard_map/transpose | solution.py:463
  125.5 0.0 copy-done.3
  125.5 0.0 copy-done.5
  125.5 7.8 %shard_map.121.refs_0_ = f32[4096,128]{1,0:T(8,128)} custom-call(bf16[4,15,32,320]{3,2,1,0:T(8,128)(2,1)S(1)} %bitcast.31, bf16[4,15,32,320]{3,2,1,0:T(8,128)(2,1)S(1)} %bitcast.29, bf16[4,15,32,320]{3,2,1,0:T(8,128)(2,1)} %get-tuple-element.19.att, bf16[4,15,32,320]{3,2,1,0:T(8,128)(2,1)} %get-tuple-element.20.qg, ...), custom_call_target="tpu_custom_call" | custom-call | flops 1572864000 | bytes 14745600 | tf_op jit(solution)/shard_map/pallas_call | solution.py:21
  133.4 1.6 copy-done.1
  135.0 42.7 %shard_map.122 = f32[4,320,320]{2,1,0:T(8,128)S(1)} custom-call(f32[4096,128]{1,0:T(8,128)S(1)} %copy-done.1), custom_call_target="tpu_custom_call" | custom-call | bytes 4194304 | tf_op jit(solution)/shard_map/pallas_call | solution.py:21
  177.7 0.0 all-to-all-done.2.back_ref
  177.7 2.2 shard_map.123
  179.9 0.0 copy-start.6
  179.9 1.1 copy-done.6
  181.0 1.1 copy.39
  182.2 2.3 collective-permute-start.2
  184.5 1.1 copy.40
  185.6 1.7 collective-permute-start.3
  187.3 1.3 slice_bitcast_fusion.2
  188.6 0.0 copy-done.7
  188.6 0.0 copy-done.10
  188.6 0.0 copy-done.12
  188.7 11.2 %shard_map.124.refs_0_ = f32[7680,128]{1,0:T(8,128)} custom-call(bf16[4,240,320]{2,1,0:T(8,128)(2,1)S(1)} %copy-done.10, bf16[4,2,240,320]{3,2,1,0:T(8,128)(2,1)S(1)} %copy-done.7, bf16[4,240,320]{2,1,0:T(8,128)(2,1)S(1)} %copy-done.12, bf16[4,2,240,320]{3,2,1,0:T(8,128)(2,1)} %copy-done.6), custom_call_target="tpu_custom_call" | custom-call | flops 3538944000 | bytes 7372800 | tf_op jit(solution)/shard_map/pallas_call | solution.py:21
  199.8 0.0 collective-permute-done.2
  199.8 0.4 copy.42.refs_1_
  200.2 0.0 collective-permute-done.3
  200.2 1.4 copy.43.refs_3_
  201.6 62.6 %shard_map.125 = (f32[9,320,320]{2,1,0:T(8,128)}, bf16[4,2,240,320]{3,2,1,0:T(8,128)(2,1)S(1)}) custom-call(f32[7680,128]{1,0:T(8,128)} %shard_map.124.refs_0_, bf16[4,240,320]{2,1,0:T(8,128)(2,1)S(1)} %copy.42.refs_1_, bf16[4,2,240,320]{3,2,1,0:T(8,128)(2,1)} %copy-done.6, bf16[4,240,320]{2,1,0:T(8,128)(2,1)S(1)} %copy.43.refs_3_, bf16[9,320,320]{2,1,0:T(8,128)(2,1)} %bitcast.36), custom_call_target="tpu_custom_call" | custom-call | bytes 16465920 | tf_op jit(solution)/shard_map/pallas_call | solution.py:21
  264.3 1.6 copy.44
  265.9 4.6 %copy.48 = f32[3,3,320,320]{3,2,1,0:T(8,128)} copy(f32[3,3,320,320]{3,2,1,0:T(8,128)} %bitcast.37) | data formatting | bytes 7372800
  (12 shorter events, 0.0 us)
Async XLA Ops:
  2.5 1.6 copy-start
  4.1 6.5 %copy-start.16 = (bf16[4,2,240,320]{2,3,1,0:T(8,128)(2,1)S(1)}, bf16[4,2,240,320]{2,3,1,0:T(8,128)(2,1)}, u32[]{:S(2)}) copy-start(bf16[4,2,240,320]{2,3,1,0:T(8,128)(2,1)} %param.7) | copy-start | bytes 3686404
  4.1 41.3 %all-to-all-start.1 = ((bf16[60,32,320]{2,1,0:T(8,128)(2,1)}), bf16[60,32,320]{2,1,0:T(8,128)(2,1)S(1)}, u32[]{:S(2)}, u32[]{:S(2)}) async-start(bf16[60,32,320]{2,1,0:T(8,128)(2,1)} %shard_map.119), calls=%async_computation.1 | async-start | bytes 2949120 | tf_op jit(solution)/shard_map/all_to_all | solution.py:408
  11.4 5.2 %collective-permute-start = (bf16[4,240,320]{1,2,0:T(8,128)(2,1)}, bf16[4,240,320]{1,2,0:T(8,128)(2,1)}, u32[]{:S(2)}, u32[]{:S(2)}) collective-permute-start(bf16[4,240,320]{1,2,0:T(8,128)(2,1)} %get-tuple-element.47), channel_id=1, source_target_pairs={{0,4},{4,8},{8,12},{12,16},{16,20},{20,24},{24,28},{1,5},{5,9},{9,... | collective-permute-start | bytes 1843208 | tf_op jit(solution)/shard_map/ppermute | solution.py:392
  13.7 4.8 %collective-permute-start.1 = (bf16[4,240,320]{1,2,0:T(8,128)(2,1)S(1)}, bf16[4,240,320]{1,2,0:T(8,128)(2,1)}, u32[]{:S(2)}, u32[]{:S(2)}) collective-permute-start(bf16[4,240,320]{1,2,0:T(8,128)(2,1)S(1)} %get-tuple-element.46), channel_id=1, source_target_pairs={{4,0},{8,4},{12,8},{16,12},{20,16},{24,20},{28,24},{5,1},{9,5},{13... | collective-permute-start | bytes 1843208 | tf_op jit(solution)/shard_map/ppermute | solution.py:392
  18.1 13.6 %copy-start.9 = (bf16[4,240,320]{2,1,0:T(8,128)(2,1)}, bf16[4,240,320]{2,1,0:T(8,128)(2,1)S(1)}, u32[]{:S(2)}) copy-start(bf16[4,240,320]{2,1,0:T(8,128)(2,1)S(1)} %copy.36.top_ref) | copy-start | bytes 1843204
  20.0 11.6 %copy-start.11 = (bf16[4,240,320]{2,1,0:T(8,128)(2,1)}, bf16[4,240,320]{2,1,0:T(8,128)(2,1)S(1)}, u32[]{:S(2)}) copy-start(bf16[4,240,320]{2,1,0:T(8,128)(2,1)S(1)} %copy.38.bottom_ref) | copy-start | bytes 1843204
  31.7 1.1 copy-start.8
  32.8 18.5 %copy-start.13 = (bf16[320,320]{1,0:T(8,128)(2,1)S(1)}, bf16[320,320]{1,0:T(8,128)(2,1)}, u32[]{:S(2)}) copy-start(bf16[320,320]{1,0:T(8,128)(2,1)} %wq.1) | copy-start | bytes 614404
  32.8 18.7 %copy-start.14 = (bf16[320,320]{1,0:T(8,128)(2,1)S(1)}, bf16[320,320]{1,0:T(8,128)(2,1)}, u32[]{:S(2)}) copy-start(bf16[320,320]{1,0:T(8,128)(2,1)} %wk.1) | copy-start | bytes 614404
  45.4 1.2 copy-start.2
  46.5 39.2 %all-to-all-start = ((bf16[60,32,320]{2,1,0:T(8,128)(2,1)}), bf16[60,32,320]{2,1,0:T(8,128)(2,1)S(1)}, u32[]{:S(2)}, u32[]{:S(2)}) async-start(bf16[60,32,320]{2,1,0:T(8,128)(2,1)} %copy-done.8), calls=%async_computation | async-start | bytes 2949120 | tf_op jit(solution)/shard_map/all_to_all | solution.py:408
  50.1 1.6 copy-start.15
  85.8 1.2 copy-start.4
  115.1 4.5 %copy-start.17 = (bf16[3,3,320,320]{3,2,1,0:T(8,128)(2,1)S(1)}, bf16[3,3,320,320]{3,2,1,0:T(8,128)(2,1)}, u32[]{:S(2)}) copy-start(bf16[3,3,320,320]{3,2,1,0:T(8,128)(2,1)} %param.9) | copy-start | bytes 5529604
  115.1 62.6 %all-to-all-start.2 = ((bf16[60,32,320]{2,1,0:T(8,128)(2,1)}), bf16[60,32,320]{2,1,0:T(8,128)(2,1)}, u32[]{:S(2)}, u32[]{:S(2)}) async-start(bf16[60,32,320]{2,1,0:T(8,128)(2,1)} %bitcast.9), calls=%async_computation.2 | async-start | bytes 2949120 | tf_op jit(solution)/shard_map/all_to_all | solution.py:408
  121.2 4.4 %copy-start.3 = (bf16[60,32,320]{2,1,0:T(8,128)(2,1)S(1)}, bf16[60,32,320]{2,1,0:T(8,128)(2,1)}, u32[]{:S(2)}) copy-start(bf16[60,32,320]{2,1,0:T(8,128)(2,1)} %copy-done.2) | copy-start | bytes 3686404
  121.2 4.4 %copy-start.5 = (bf16[60,32,320]{2,1,0:T(8,128)(2,1)S(1)}, bf16[60,32,320]{2,1,0:T(8,128)(2,1)}, u32[]{:S(2)}) copy-start(bf16[60,32,320]{2,1,0:T(8,128)(2,1)} %copy-done.4) | copy-start | bytes 3686404
  133.4 1.6 copy-start.1
  179.9 1.2 copy-start.6
  182.2 17.7 %collective-permute-start.2 = (bf16[4,240,320]{1,2,0:T(8,128)(2,1)}, bf16[4,240,320]{1,2,0:T(8,128)(2,1)S(1)}, u32[]{:S(2)}, u32[]{:S(2)}) collective-permute-start(bf16[4,240,320]{1,2,0:T(8,128)(2,1)} %copy.39), channel_id=1, source_target_pairs={{0,4},{4,8},{8,12},{12,16},{16,20},{20,24},{24,28},{1,5},{5,9},{9,... | collective-permute-start | bytes 1843208 | tf_op jit(solution)/shard_map/ppermute | solution.py:392
  185.6 3.0 %copy-start.7 = (bf16[4,2,240,320]{3,2,1,0:T(8,128)(2,1)S(1)}, bf16[4,2,240,320]{3,2,1,0:T(8,128)(2,1)}, u32[]{:S(2)}) copy-start(bf16[4,2,240,320]{3,2,1,0:T(8,128)(2,1)} %copy.37.cells_ref) | copy-start | bytes 3686404
  185.6 3.0 %copy-start.10 = (bf16[4,240,320]{2,1,0:T(8,128)(2,1)S(1)}, bf16[4,240,320]{2,1,0:T(8,128)(2,1)}, u32[]{:S(2)}) copy-start(bf16[4,240,320]{2,1,0:T(8,128)(2,1)} %copy-done.9) | copy-start | bytes 1843204
  185.6 3.0 %copy-start.12 = (bf16[4,240,320]{2,1,0:T(8,128)(2,1)S(1)}, bf16[4,240,320]{2,1,0:T(8,128)(2,1)}, u32[]{:S(2)}) copy-start(bf16[4,240,320]{2,1,0:T(8,128)(2,1)} %copy-done.11) | copy-start | bytes 1843204
  185.6 14.6 %collective-permute-start.3 = (bf16[4,240,320]{1,2,0:T(8,128)(2,1)}, bf16[4,240,320]{1,2,0:T(8,128)(2,1)}, u32[]{:S(2)}, u32[]{:S(2)}) collective-permute-start(bf16[4,240,320]{1,2,0:T(8,128)(2,1)} %copy.40), channel_id=1, source_target_pairs={{4,0},{8,4},{12,8},{16,12},{20,16},{24,20},{28,24},{5,1},{9,5},{13... | collective-permute-start | bytes 1843208 | tf_op jit(solution)/shard_map/ppermute | solution.py:392

commit v3 on v2

--- a/solution.py
+++ b/solution.py
@@ -71,16 +71,32 @@
     return cat.astype(BF16)
 
 
-def regroup_kernel(cells_ref, out_ref):
+def fill(out_ref, cells, start):
+    count = min(out_ref.shape[0], cells.shape[0] - start)
+    if count > 0:
+        out_ref[0:count] = cells[start : start + count]
+    if out_ref.shape[0] > count:
+        out_ref[count:] = jnp.zeros((out_ref.shape[0] - count,) + out_ref.shape[1:], BF16)
+
+
+def regroup_kernel(halves, cells_ref, out_ref):
     frames, rows, cols, chans = cells_ref.shape
     real = rows * cols // PIXEL_BLOCK
     parts = [cells_ref[f].reshape(rows * cols, chans).astype(F32) for f in range(frames)]
-    out_ref[0:real] = regroup(parts, real)
-    if out_ref.shape[0] > real:
-        out_ref[real:] = jnp.zeros((out_ref.shape[0] - real,) + out_ref.shape[1:], BF16)
-
-
-def conv_kernel(top_ref, cells_ref, bottom_ref, weight_ref, out_ref, ext, pad, held):
+    cells = regroup(parts, real)
+    per = sum(halves)
+    owners = out_ref.shape[0] // per
+    first = halves[0] * owners
+    for owner in range(owners):
+        at = owner * per
+        for start, length, base in (
+            (owner * halves[0], halves[0], 0),
+            (first + owner * halves[1], halves[1], halves[0]),
+        ):
+            fill(out_ref.at[at + base : at + base + length], cells, min(start, real))
+
+
+def conv_kernel(top_ref, cells_ref, bottom_ref, weight_ref, one_ref, two_ref, ext, pad, held):
     frames, rows, cols, chans = cells_ref.shape
 
     def one_frame(f, carry):
@@ -89,16 +105,16 @@
 
     lax.fori_loop(0, frames, one_frame, 0)
     real = rows * cols // PIXEL_BLOCK
-    out_ref[0:real] = regroup([held[f] for f in range(frames)], real)
-    if out_ref.shape[0] > real:
-        out_ref[real:] = jnp.zeros((out_ref.shape[0] - real,) + out_ref.shape[1:], BF16)
-
-
-def convolve(top, cells, bottom, weight, groups):
+    cells = regroup([held[f] for f in range(frames)], real)
+    fill(one_ref, cells, 0)
+    fill(two_ref, cells, one_ref.shape[0])
+
+
+def convolve(top, cells, bottom, weight, counts):
     frames, rows, cols, chans = cells.shape
     return call(
         conv_kernel,
-        shape_of((groups, frames * PIXEL_BLOCK, chans), BF16),
+        tuple(shape_of((count, frames * PIXEL_BLOCK, chans), BF16) for count in counts),
         (top, cells, bottom, weight),
         conv_scratch(rows, cols, chans) + [pltpu.VMEM((frames, rows * cols, chans), F32)],
         flops=18 * cells.size * chans,
@@ -106,7 +122,7 @@
 
 
 def attend_kernel(
-    hid, cot, wq, wk, wv, wot, wqt, wkt, wvt, cols_o, att_o, qg_o, kg_o, vg_o, q_s, k_s, v_s, g_s
+    base, hid, cot, wq, wk, wv, wot, wqt, wkt, wvt, cols_o, att_o, qg_o, kg_o, vg_o, q_s, k_s, v_s, g_s
 ):
     sources, groups, span, chans = hid.shape
     heads = chans // HEAD_DIM
@@ -118,7 +134,7 @@
         h = hid[t].reshape(flat, chans)
         for ref, w in ((q_s, wq), (k_s, wk), (v_s, wv)):
             ref[t] = dot(h, w[...]).astype(BF16).reshape(groups, span, chans)
-        c = cot[t].reshape(flat, chans)
+        c = cot[t, base : base + groups].reshape(flat, chans)
         g_s[t] = dot(c, wot[...]).astype(BF16).reshape(groups, span, chans)
         return carry
 
@@ -211,26 +227,32 @@
     return -(-pack_places(count, chans)[1] // unit) * devices * 16
 
 
-def weight_grads_kernel(hid, cot, att, qg, kg, vg, out_ref, total):
-    sources, groups, span, chans = hid.shape
-    flat = groups * span
+def weight_grads_kernel(cot, *refs):
+    halves, (out_ref, total) = (refs[0:5], refs[5:10]), refs[10:]
     total[...] = jnp.zeros(total.shape, F32)
 
     def one(t, carry):
-        ht = hid[t].reshape(flat, chans).T
-        for i, ref in enumerate((qg, kg, vg)):
-            total[i] += dot(ht, ref[t].reshape(flat, chans))
-        total[3] += dot(att[t].reshape(flat, chans).T, cot[t].reshape(flat, chans))
+        base = 0
+        for hid, att, qg, kg, vg in halves:
+            _, groups, span, chans = hid.shape
+            flat = groups * span
+            ht = hid[t].reshape(flat, chans).T
+            for i, ref in enumerate((qg, kg, vg)):
+                total[i] += dot(ht, ref[t].reshape(flat, chans))
+            c = cot[t, base : base + groups].reshape(flat, chans)
+            total[3] += dot(att[t].reshape(flat, chans).T, c)
+            base += groups
         return carry
 
-    lax.fori_loop(0, sources, one, 0)
+    lax.fori_loop(0, cot.shape[0], one, 0)
     pack(total, out_ref)
 
 
-def hidden_grad_kernel(back_ref, cot_ref, out_ref, first_ref, last_ref):
+def hidden_grad_kernel(one_ref, two_ref, cot_ref, out_ref, first_ref, last_ref):
     frames, rows, cols, chans = cot_ref.shape
     real = rows * cols // PIXEL_BLOCK
-    back = back_ref[0:real].astype(F32)
+    rest = real - one_ref.shape[0]
+    back = jnp.concatenate([one_ref[...].astype(F32), two_ref[0:rest].astype(F32)], axis=0)
     for f in range(frames):
         piece = back[:, f * PIXEL_BLOCK : (f + 1) * PIXEL_BLOCK].reshape(rows, cols, chans)
         total = (cot_ref[f].astype(F32) + piece).astype(BF16)
@@ -283,7 +305,7 @@
     return plan, first + planes + line
 
 
-def reduce_kernel(plan, greet, part_rows, norm, beside, *refs):
+def reduce_kernel(plan, greet, part_rows, beside, *refs):
     if beside:
         x_ref, top_ref, cells_ref, bottom_ref, weight_ref, out_ref, result_ref = refs[:7]
         ext, pad, acc, low, send_sems, recv_sems, *recvs = refs[7:]
@@ -354,16 +376,20 @@
         for copy in copies:
             copy.wait()
         offs, size = wider, size * 2
+    out_ref[...] = low[...]
+
+
+def unpack_kernel(norm, packed_ref, out_ref):
     count, chans, _ = out_ref.shape
     for row, lane, m, col, width in pack_places(count, chans)[0]:
-        piece = low[row : row + chans, lane : lane + width].astype(F32)
+        piece = packed_ref[row : row + chans, lane : lane + width].astype(F32)
         out_ref[m, :, col : col + width] = piece * norm
 
 
 def total_over_devices(arr, count, chans, norm, sizes, parts, part_rows, links_first, number, conv=()):
     plan, greet = hops(sizes, parts, links_first)
     steps = len(greet)
-    out = shape_of((count, chans, chans), F32)
+    out = shape_of(arr.shape, BF16)
     scratch = []
     if conv:
         out = (out, shape_of(conv[1].shape, BF16))
@@ -375,14 +401,19 @@
         pltpu.SemaphoreType.DMA((2 * steps, parts)),
     ]
     scratch += [pltpu.VMEM((parts, part_rows >> (s + 1), LANES), F32) for s in range(steps)]
-    return call(
-        functools.partial(reduce_kernel, plan, greet, part_rows, norm, bool(conv)),
+    result = call(
+        functools.partial(reduce_kernel, plan, greet, part_rows, bool(conv)),
         out,
         (arr,) + conv,
         scratch,
         collective_id=number,
         has_side_effects=True,
     )
+    packed = result[0] if conv else result
+    grads = call(
+        functools.partial(unpack_kernel, norm), shape_of((count, chans, chans), F32), (packed,)
+    )
+    return (grads, result[1]) if conv else grads
 
 
 def halo(first, last):
@@ -402,46 +433,56 @@
     per_source = -(-(rows * cols // PIXEL_BLOCK) // tm)
     groups = per_source * tm
     span = frames * PIXEL_BLOCK
-    grouped = (tm, per_source, span, chans)
+    halves = (-(-per_source // 2), per_source // 2)
 
     def exchange(arr):
         return lax.all_to_all(arr, "tm", split_axis=0, concat_axis=0, tiled=True)
 
+    def owned(arr, count):
+        return exchange(arr).reshape(tm, count, span, chans)
+
     top, bottom = halo(latents[:, 0], latents[:, rows - 1])
-    cot_groups = call(regroup_kernel, shape_of((groups, span, chans), BF16), (cotangent,))
-    cot_all = exchange(cot_groups).reshape(grouped)
+    cot_groups = call(
+        functools.partial(regroup_kernel, halves),
+        shape_of((groups, span, chans), BF16),
+        (cotangent,),
+    )
+    cot_all = owned(cot_groups, per_source)
     weights = conv_weight.reshape(9, chans, chans)
-    hidden = convolve(top, latents, bottom, weights, groups)
-    hid_all = exchange(hidden).reshape(grouped)
-    tile = shape_of(grouped, BF16)
-    attn_cols, attended, query_grad, key_grad, value_grad = call(
-        attend_kernel,
-        (tile,) * 5,
-        (
-            hid_all,
-            cot_all,
-            query_weight,
-            key_weight,
-            value_weight,
-            out_weight.T,
-            query_weight.T,
-            key_weight.T,
-            value_weight.T,
-        ),
-        [pltpu.VMEM(grouped, BF16)] * 4,
-        flops=20 * hid_all.size * chans,
-    )
-    attn_back = exchange(attn_cols.reshape(groups, span, chans))
+    hidden = convolve(top, latents, bottom, weights, [tm * half for half in halves])
+    backs, saved = [], []
+    for i, half in enumerate(halves):
+        hid = owned(hidden[i], half)
+        tile = shape_of(hid.shape, BF16)
+        attn_cols, *grads = call(
+            functools.partial(attend_kernel, i * halves[0]),
+            (tile,) * 5,
+            (
+                hid,
+                cot_all,
+                query_weight,
+                key_weight,
+                value_weight,
+                out_weight.T,
+                query_weight.T,
+                key_weight.T,
+                value_weight.T,
+            ),
+            [pltpu.VMEM(hid.shape, BF16)] * 4,
+            flops=20 * hid.size * chans,
+        )
+        backs.append(exchange(attn_cols.reshape(tm * half, span, chans)))
+        saved += [hid] + grads
     small_rows = part_size(4, chans, 2, devices)
     small = call(
         weight_grads_kernel,
         shape_of((2 * small_rows, LANES), F32),
-        (hid_all, cot_all, attended, query_grad, key_grad, value_grad),
+        (cot_all, *saved),
         [pltpu.VMEM((4, chans, chans), F32)],
-        flops=8 * hid_all.size * chans,
+        flops=8 * cot_all.size * chans,
     )
     small = total_over_devices(small, 4, chans, norm, sizes, 2, small_rows, True, 0)
-    attn_back, small = lax.optimization_barrier((attn_back, small))
+    backs, small = lax.optimization_barrier((backs, small))
     hidden_grad, first, last = call(
         hidden_grad_kernel,
         (
@@ -449,7 +490,7 @@
             shape_of((frames, cols, chans), BF16),
             shape_of((frames, cols, chans), BF16),
         ),
-        (attn_back, cotangent),
+        (*backs, cotangent),
     )
     grad_top, grad_bottom = halo(first, last)
     part_rows = part_size(9, chans, 3, devices)

time: 271 us -> 305 us (1.13)
  waiting for transfers between devices: 46.9 us -> 12.9 us
  Pallas kernels: 168 us -> 201 us
  blocking collectives: 0 us -> 29.8 us
  starting transfers between devices: 22.1 us -> 27.4 us
    all_to_all x3 -> x4, waiting for transfers between devices: 46.4 us -> 11.9 us  [exchange(): return lax.all_to_all(arr, 'tm', split_axis=0, concat_axis=0, tiled=True)]
    pallas_call x8 -> x11, Pallas kernels: 168 us -> 201 us  [call(): pl.pallas_call(body, out_shape=out_shape, in_specs=[pl.BlockSpec(memory_s...]
    all_to_all x0 -> x1, blocking collectives: none -> 29.8 us  [exchange(): return lax.all_to_all(arr, 'tm', split_axis=0, concat_axis=0, tiled=True)]
    all_to_all x3 -> x4, starting transfers between devices: 14.5 us -> 19.1 us  [exchange(): return lax.all_to_all(arr, 'tm', split_axis=0, concat_axis=0, tiled=True)]
    unnamed x44 -> x57, local copies, waits for them, and re-layouts: 17.8 us -> 14.9 us
  transfers between devices with their start and end apart: 7 -> 8, of which waited for: 3 -> 3; matrix products, arithmetic and copies ran while one was open for 6% -> 6% of each run, Pallas kernels for 27% -> 39%
where the time goes in v3:
time: 305 us; the launch traced here: 304 us
  Pallas kernels  201 us (66%)
  local copies, waits for them, and re-layouts  32.4 us (11%)
  blocking collectives  29.8 us (10%)
  starting transfers between devices  27.4 us (9%)
  waiting for transfers between devices  12.9 us (4%)
    pallas_call x11, Pallas kernels, call(): pl.pallas_call(body, out_shape=out_shape, in_specs=[pl.BlockSpec(memory_s...  201 us
    all_to_all x1, blocking collectives, exchange(): return lax.all_to_all(arr, 'tm', split_axis=0, concat_axis=0, tiled=True)  29.8 us
    all_to_all x4, starting transfers between devices, exchange(): return lax.all_to_all(arr, 'tm', split_axis=0, concat_axis=0, tiled=True)  19.1 us
    unnamed x57, local copies, waits for them, and re-layouts  14.9 us
    all_to_all x4, waiting for transfers between devices, exchange(): return lax.all_to_all(arr, 'tm', split_axis=0, concat_axis=0, tiled=True)  11.9 us
    ppermute x4, starting transfers between devices, halo(): return (lax.ppermute(last, 'space', up), lax.ppermute(first, 'space', down))  8.34 us
    transpose x2, local copies, waits for them, and re-layouts, on_device(): jnp.swapaxes(conv_weight[::-1, ::-1], 2, 3).reshape(9, chans, chans)  7.5 us
  transfers between devices with their start and end apart: 8, of which 3 were waited for; matrix products, arithmetic and copies ran while one was open for 6% of the time, Pallas kernels for 39%

profile of v3, /device:TPU:0, one launch (start us, length us, event | category | flops | bytes accessed | tf_op | source)
XLA Modules:
  0.0 304.1 jit_solution(11876966228426950854)
XLA Ops:
  0.6 0.0 copy-start.23
  0.6 1.5 slice_bitcast_fusion
  2.1 3.2 %collective-permute-start = (bf16[4,240,320]{1,2,0:T(8,128)(2,1)S(1)}, bf16[4,240,320]{1,2,0:T(8,128)(2,1)}, u32[]{:S(2)}, u32[]{:S(2)}) collective-permute-start(bf16[4,240,320]{1,2,0:T(8,128)(2,1)S(1)} %get-tuple-element.63), channel_id=1, source_target_pairs={{0,4},{4,8},{8,12},{12,16},{16,20},{20,24},{24,28},{1,5},{5,9},{9,... | collective-permute-start | bytes 1843208 | tf_op jit(solution)/shard_map/ppermute | solution.py:423
  5.3 1.3 collective-permute-start.1
  6.6 0.0 copy-done.23
  6.6 1.5 copy.37.cells_ref
  8.2 0.0 collective-permute-done
  8.2 1.4 copy.36.top_ref
  9.6 1.0 collective-permute-done.1
  10.6 0.4 copy.38.bottom_ref
  11.0 12.4 %shard_map.118 = (bf16[32,32,320]{2,1,0:T(8,128)(2,1)S(1)}, bf16[28,32,320]{2,1,0:T(8,128)(2,1)}) custom-call(bf16[4,240,320]{2,1,0:T(8,128)(2,1)S(1)} %copy.36.top_ref, bf16[4,2,240,320]{3,2,1,0:T(8,128)(2,1)} %copy.37.cells_ref, bf16[4,240,320]{2,1,0:T(8,128)(2,1)S(1)} %copy.38.bottom_ref, bf16[9,320,320]{2,1,0:T(8,128)(2,1)} %bitcast.43), custom_call_target="tpu_custom_call" | custom-call | flops 3538944000 | bytes 8601600 | tf_op jit(solution)/shard_map/pallas_call | solution.py:21
  23.3 0.0 copy-done.7
  23.3 0.9 copy-done.4
  24.2 5.0 %all-to-all-start.3 = ((bf16[28,32,320]{2,1,0:T(8,128)(2,1)}), bf16[28,32,320]{2,1,0:T(8,128)(2,1)}, u32[]{:S(2)}, u32[]{:S(2)}) async-start(bf16[28,32,320]{2,1,0:T(8,128)(2,1)} %get-tuple-element.28), calls=%async_computation.3 | async-start | bytes 1376256 | tf_op jit(solution)/shard_map/all_to_all | solution.py:439
  29.2 0.0 copy-done.24
  29.2 0.8 copy.30.cells_ref.cot_ref
  30.1 0.0 copy-start
  30.1 0.1 shard_map.119
  30.2 0.0 copy-start.15
  30.2 11.1 %all-to-all-done.3 = bf16[28,32,320]{2,1,0:T(8,128)(2,1)} async-done(((bf16[28,32,320]{2,1,0:T(8,128)(2,1)}), bf16[28,32,320]{2,1,0:T(8,128)(2,1)}, u32[]{:S(2)}, u32[]{:S(2)}) %all-to-all-start.3) | async-done | bytes 573472 | tf_op jit(solution)/shard_map/all_to_all | solution.py:439
  41.4 29.8 %all_to_all.25 = bf16[60,32,320]{2,1,0:T(8,128)(2,1)} all-to-all(bf16[60,32,320]{2,1,0:T(8,128)(2,1)S(1)} %shard_map.119), channel_id=1, replica_groups=mesh['space'=8,'tm'=4] {'tm'}, dimensions={0} | all-to-all | bytes 2457600 | tf_op jit(solution)/shard_map/all_to_all | solution.py:439
  71.2 4.6 %all-to-all-start = ((bf16[32,32,320]{2,1,0:T(8,128)(2,1)}), bf16[32,32,320]{2,1,0:T(8,128)(2,1)}, u32[]{:S(2)}, u32[]{:S(2)}) async-start(bf16[32,32,320]{2,1,0:T(8,128)(2,1)} %copy-done.4), calls=%async_computation | async-start | bytes 1572864 | tf_op jit(solution)/shard_map/all_to_all | solution.py:439
  75.8 1.1 copy.31
  76.9 0.2 copy.32
  77.1 0.2 copy.33
  77.3 0.0 copy-start.19
  77.4 0.2 copy.34
  77.6 0.0 copy-start.21
  77.6 0.0 copy-done.18
  77.6 14.5 %shard_map.121 = (bf16[4,7,32,320]{3,2,1,0:T(8,128)(2,1)}, bf16[4,7,32,320]{3,2,1,0:T(8,128)(2,1)S(1)}, bf16[4,7,32,320]{3,2,1,0:T(8,128)(2,1)S(1)}, bf16[4,7,32...) custom-call(bf16[4,7,32,320]{3,2,1,0:T(8,128)(2,1)} %bitcast.10.hid.refs_5_, bf16[4,15,32,320]{3,2,1,0:T(8,128)(2,1)} %bitcast.39, ...), custom_call_target="tpu_custom_call" | custom-call | flops 1835008000 | bytes 6471680 | tf_op jit(solution)/shard_map/pallas_call | solution.py:21
  92.1 0.7 all-to-all-done
  92.8 4.4 %all-to-all-start.4 = ((bf16[28,32,320]{2,1,0:T(8,128)(2,1)}), bf16[28,32,320]{2,1,0:T(8,128)(2,1)S(1)}, u32[]{:S(2)}, u32[]{:S(2)}) async-start(bf16[28,32,320]{2,1,0:T(8,128)(2,1)} %bitcast.11), calls=%async_computation.4 | async-start | bytes 1376256 | tf_op jit(solution)/shard_map/all_to_all | solution.py:439
  97.2 0.9 copy-done.20
  98.1 0.9 copy-done.22
  99.1 16.1 %shard_map.120 = (bf16[4,8,32,320]{3,2,1,0:T(8,128)(2,1)}, bf16[4,8,32,320]{3,2,1,0:T(8,128)(2,1)S(1)}, bf16[4,8,32,320]{3,2,1,0:T(8,128)(2,1)S(1)}, bf16[4,8,32...) custom-call(bf16[4,8,32,320]{3,2,1,0:T(8,128)(2,1)} %bitcast.3.hid.refs_0_, bf16[4,15,32,320]{3,2,1,0:T(8,128)(2,1)} %bitcast.40, ...), custom_call_target="tpu_custom_call" | custom-call | flops 2097152000 | bytes 6635520 | tf_op jit(solution)/shard_map/pallas_call | solution.py:21
  115.2 0.9 copy-done.5
  116.0 0.9 copy-done.6
  116.9 0.0 all-to-all-done.4.two_ref
  116.9 5.1 %all-to-all-start.2 = ((bf16[32,32,320]{2,1,0:T(8,128)(2,1)}), bf16[32,32,320]{2,1,0:T(8,128)(2,1)S(1)}, u32[]{:S(2)}, u32[]{:S(2)}) async-start(bf16[32,32,320]{2,1,0:T(8,128)(2,1)} %bitcast.9), calls=%async_computation.2 | async-start | bytes 1572864 | tf_op jit(solution)/shard_map/all_to_all | solution.py:439
  122.0 3.2 %reverse_bitcast_fusion = bf16[3,3,320,320]{2,3,1,0:T(8,128)(2,1)} fusion(bf16[3,3,320,320]{3,2,1,0:T(8,128)(2,1)} %param.9), kind=kLoop, calls=%fused_computation | loop fusion | bytes 3686400 | tf_op jit(solution)/shard_map/transpose | solution.py:504
  125.2 4.3 %copy.41 = bf16[3,3,320,320]{3,2,1,0:T(8,128)(2,1)} copy(bf16[3,3,320,320]{2,3,1,0:T(8,128)(2,1)} %reverse_bitcast_fusion) | data formatting | bytes 3686400 | tf_op jit(solution)/shard_map/transpose | solution.py:504
  129.5 1.1 copy-done.14
  130.6 7.9 %shard_map.122.refs_0_ = f32[4096,128]{1,0:T(8,128)} custom-call(bf16[4,15,32,320]{3,2,1,0:T(8,128)(2,1)} %bitcast.41, bf16[4,8,32,320]{3,2,1,0:T(8,128)(2,1)} %bitcast.3.hid.refs_0_, bf16[4,8,32,320]{3,2,1,0:T(8,128)(2,1)} %copy-done.5, bf16[4,8,32,320]{3,2,1,0:T(8,128)(2,1)} %copy-done.6, bf16[4,8,32,320]{3,2,1,0:T(8,128)(2,1)} %get-tuple-element.32.refs_3_, ...), custom_call_target="tpu_custom_call" | custom-call | flops 1572864000 | bytes 14745600 | tf_op jit(solution)/shard_map/pallas_call | solution.py:21
  138.5 1.6 copy-done.1
  140.1 69.4 %shard_map.123.packed_ref = bf16[4096,128]{1,0:T(8,128)(2,1)S(1)} custom-call(f32[4096,128]{1,0:T(8,128)S(1)} %copy-done.1), custom_call_target="tpu_custom_call" | custom-call | bytes 4194304 | tf_op jit(solution)/shard_map/pallas_call | solution.py:21
  209.5 0.2 shard_map.124
  209.8 0.0 all-to-all-done.2.one_ref
  209.8 2.9 shard_map.125
  212.7 0.9 copy-done.11
  213.5 0.9 copy-done.12
  214.4 1.4 copy.39
  215.8 2.3 collective-permute-start.2
  218.1 2.2 copy.40
  220.3 1.5 collective-permute-start.3
  221.9 1.3 slice_bitcast_fusion.2
  223.2 11.2 %shard_map.126.refs_0_ = f32[7680,128]{1,0:T(8,128)} custom-call(bf16[4,240,320]{2,1,0:T(8,128)(2,1)S(1)} %copy-done.8, bf16[4,2,240,320]{3,2,1,0:T(8,128)(2,1)S(1)} %copy-done.3, bf16[4,240,320]{2,1,0:T(8,128)(2,1)S(1)} %copy-done.10, bf16[4,2,240,320]{3,2,1,0:T(8,128)(2,1)} %get-tuple-element.40.grad_ref.refs_2_), custom_call_target="tpu_custom_call" | custom-call | flops 3538944000 | bytes 7372800 | tf_op jit(solution)/shard_map/pallas_call | solution.py:21
  234.4 0.0 collective-permute-done.2
  234.4 0.4 copy.42.refs_1_
  234.7 0.0 collective-permute-done.3
  234.7 1.4 copy.43.refs_3_
  236.2 63.6 %shard_map.127 = (bf16[7680,128]{1,0:T(8,128)(2,1)}, bf16[4,2,240,320]{3,2,1,0:T(8,128)(2,1)S(1)}) custom-call(f32[7680,128]{1,0:T(8,128)} %shard_map.126.refs_0_, bf16[4,240,320]{2,1,0:T(8,128)(2,1)S(1)} %copy.42.refs_1_, bf16[4,2,240,320]{3,2,1,0:T(8,128)(2,1)} %get-tuple-element.40.grad_ref.refs_2_, bf16[4,240,320]{2,1,0:T(8,128)(2,1)S(1)} %copy.43.refs_3_, ...), custom_call_target="tpu_custom_call" | custom-call | bytes 16465920 | tf_op jit(solution)/shard_map/pallas_call | solution.py:21
  299.8 1.6 copy.44
  301.3 0.3 copy-done.2
  301.6 2.5 shard_map.128
  (31 shorter events, 0.1 us)
Async XLA Ops:
  0.6 6.0 %copy-start.23 = (bf16[4,2,240,320]{2,3,1,0:T(8,128)(2,1)S(1)}, bf16[4,2,240,320]{2,3,1,0:T(8,128)(2,1)}, u32[]{:S(2)}) copy-start(bf16[4,2,240,320]{2,3,1,0:T(8,128)(2,1)} %param.7) | copy-start | bytes 3686404
  2.1 6.0 %collective-permute-start = (bf16[4,240,320]{1,2,0:T(8,128)(2,1)S(1)}, bf16[4,240,320]{1,2,0:T(8,128)(2,1)}, u32[]{:S(2)}, u32[]{:S(2)}) collective-permute-start(bf16[4,240,320]{1,2,0:T(8,128)(2,1)S(1)} %get-tuple-element.63), channel_id=1, source_target_pairs={{0,4},{4,8},{8,12},{12,16},{16,20},{20,24},{24,28},{1,5},{5,9},{9,... | collective-permute-start | bytes 1843208 | tf_op jit(solution)/shard_map/ppermute | solution.py:423
  5.3 5.3 %collective-permute-start.1 = (bf16[4,240,320]{1,2,0:T(8,128)(2,1)S(1)}, bf16[4,240,320]{1,2,0:T(8,128)(2,1)S(1)}, u32[]{:S(2)}, u32[]{:S(2)}) collective-permute-start(bf16[4,240,320]{1,2,0:T(8,128)(2,1)S(1)} %get-tuple-element.62), channel_id=1, source_target_pairs={{4,0},{8,4},{12,8},{16,12},{20,16},{24,20},{28,24},{5,1},{9,5},{13... | collective-permute-start | bytes 1843208 | tf_op jit(solution)/shard_map/ppermute | solution.py:423
  9.6 13.7 %copy-start.7 = (bf16[4,240,320]{2,1,0:T(8,128)(2,1)}, bf16[4,240,320]{2,1,0:T(8,128)(2,1)S(1)}, u32[]{:S(2)}) copy-start(bf16[4,240,320]{2,1,0:T(8,128)(2,1)S(1)} %copy.36.top_ref) | copy-start | bytes 1843204
  10.9 12.4 %copy-start.9 = (bf16[4,240,320]{2,1,0:T(8,128)(2,1)}, bf16[4,240,320]{2,1,0:T(8,128)(2,1)S(1)}, u32[]{:S(2)}) copy-start(bf16[4,240,320]{2,1,0:T(8,128)(2,1)S(1)} %copy.38.bottom_ref) | copy-start | bytes 1843204
  23.3 0.9 copy-start.4
  24.2 5.0 %copy-start.24 = (bf16[4,2,240,320]{2,3,1,0:T(8,128)(2,1)S(1)}, bf16[4,2,240,320]{2,3,1,0:T(8,128)(2,1)}, u32[]{:S(2)}) copy-start(bf16[4,2,240,320]{2,3,1,0:T(8,128)(2,1)} %param.8) | copy-start | bytes 3686404
  24.2 17.2 %all-to-all-start.3 = ((bf16[28,32,320]{2,1,0:T(8,128)(2,1)}), bf16[28,32,320]{2,1,0:T(8,128)(2,1)}, u32[]{:S(2)}, u32[]{:S(2)}) async-start(bf16[28,32,320]{2,1,0:T(8,128)(2,1)} %get-tuple-element.28), calls=%async_computation.3 | async-start | bytes 1376256 | tf_op jit(solution)/shard_map/all_to_all | solution.py:439
  30.1 41.1 %copy-start = (bf16[4,2,240,320]{3,2,1,0:T(8,128)(2,1)}, bf16[4,2,240,320]{3,2,1,0:T(8,128)(2,1)S(1)}, u32[]{:S(2)}) copy-start(bf16[4,2,240,320]{3,2,1,0:T(8,128)(2,1)S(1)} %copy.30.cells_ref.cot_ref) | copy-start | bytes 3686404
  30.2 46.7 %copy-start.15 = (bf16[320,320]{1,0:T(8,128)(2,1)S(1)}, bf16[320,320]{1,0:T(8,128)(2,1)}, u32[]{:S(2)}) copy-start(bf16[320,320]{1,0:T(8,128)(2,1)} %wq.3) | copy-start | bytes 614404
  71.2 6.0 %copy-start.16 = (bf16[320,320]{1,0:T(8,128)(2,1)S(1)}, bf16[320,320]{1,0:T(8,128)(2,1)}, u32[]{:S(2)}) copy-start(bf16[320,320]{1,0:T(8,128)(2,1)} %wk.3) | copy-start | bytes 614404
  71.2 6.2 %copy-start.17 = (bf16[320,320]{1,0:T(8,128)(2,1)S(1)}, bf16[320,320]{1,0:T(8,128)(2,1)}, u32[]{:S(2)}) copy-start(bf16[320,320]{1,0:T(8,128)(2,1)} %wv.3) | copy-start | bytes 614404
  71.2 6.4 %copy-start.18 = (bf16[320,320]{1,0:T(8,128)(2,1)S(1)}, bf16[320,320]{1,0:T(8,128)(2,1)}, u32[]{:S(2)}) copy-start(bf16[320,320]{1,0:T(8,128)(2,1)} %wv.3) | copy-start | bytes 614404
  71.2 21.7 %all-to-all-start = ((bf16[32,32,320]{2,1,0:T(8,128)(2,1)}), bf16[32,32,320]{2,1,0:T(8,128)(2,1)}, u32[]{:S(2)}, u32[]{:S(2)}) async-start(bf16[32,32,320]{2,1,0:T(8,128)(2,1)} %copy-done.4), calls=%async_computation | async-start | bytes 1572864 | tf_op jit(solution)/shard_map/all_to_all | solution.py:439
  77.3 14.8 %copy-start.19 = (bf16[320,320]{0,1:T(8,128)(2,1)}, bf16[320,320]{0,1:T(8,128)(2,1)S(1)}, u32[]{:S(2)}) copy-start(bf16[320,320]{0,1:T(8,128)(2,1)S(1)} %copy.33) | copy-start | bytes 614404
  77.6 14.5 %copy-start.21 = (bf16[320,320]{0,1:T(8,128)(2,1)}, bf16[320,320]{0,1:T(8,128)(2,1)S(1)}, u32[]{:S(2)}) copy-start(bf16[320,320]{0,1:T(8,128)(2,1)S(1)} %copy.34) | copy-start | bytes 614404
  92.8 24.1 %all-to-all-start.4 = ((bf16[28,32,320]{2,1,0:T(8,128)(2,1)}), bf16[28,32,320]{2,1,0:T(8,128)(2,1)S(1)}, u32[]{:S(2)}, u32[]{:S(2)}) async-start(bf16[28,32,320]{2,1,0:T(8,128)(2,1)} %bitcast.11), calls=%async_computation.4 | async-start | bytes 1376256 | tf_op jit(solution)/shard_map/all_to_all | solution.py:439
  97.2 0.9 copy-start.20
  98.1 0.9 copy-start.22
  115.2 0.9 copy-start.5
  116.0 0.9 copy-start.6
  116.9 92.8 %all-to-all-start.2 = ((bf16[32,32,320]{2,1,0:T(8,128)(2,1)}), bf16[32,32,320]{2,1,0:T(8,128)(2,1)S(1)}, u32[]{:S(2)}, u32[]{:S(2)}) async-start(bf16[32,32,320]{2,1,0:T(8,128)(2,1)} %bitcast.9), calls=%async_computation.2 | async-start | bytes 1572864 | tf_op jit(solution)/shard_map/all_to_all | solution.py:439
  125.2 4.3 %copy-start.13 = (bf16[4,7,32,320]{3,2,1,0:T(8,128)(2,1)S(1)}, bf16[4,7,32,320]{3,2,1,0:T(8,128)(2,1)}, u32[]{:S(2)}) copy-start(bf16[4,7,32,320]{3,2,1,0:T(8,128)(2,1)} %get-tuple-element.36.refs_8_) | copy-start | bytes 1720324
  129.5 1.1 copy-start.14
  138.5 1.6 copy-start.1
  212.7 0.9 copy-start.11
  213.5 0.9 copy-start.12
  215.8 18.6 %collective-permute-start.2 = (bf16[4,240,320]{1,2,0:T(8,128)(2,1)S(1)}, bf16[4,240,320]{1,2,0:T(8,128)(2,1)S(1)}, u32[]{:S(2)}, u32[]{:S(2)}) collective-permute-start(bf16[4,240,320]{1,2,0:T(8,128)(2,1)S(1)} %copy.39), channel_id=1, source_target_pairs={{0,4},{4,8},{8,12},{12,16},{16,20},{20,24},{24,28},{1,5},{5,9},{9,... | collective-permute-start | bytes 1843208 | tf_op jit(solution)/shard_map/ppermute | solution.py:423
  220.3 2.9 copy-start.3
  220.3 2.9 copy-start.8
  220.3 2.9 copy-start.10
  220.3 14.4 %collective-permute-start.3 = (bf16[4,240,320]{1,2,0:T(8,128)(2,1)}, bf16[4,240,320]{1,2,0:T(8,128)(2,1)}, u32[]{:S(2)}, u32[]{:S(2)}) collective-permute-start(bf16[4,240,320]{1,2,0:T(8,128)(2,1)} %copy.40), channel_id=1, source_target_pairs={{4,0},{8,4},{12,8},{16,12},{20,16},{24,20},{28,24},{5,1},{9,5},{13... | collective-permute-start | bytes 1843208 | tf_op jit(solution)/shard_map/ppermute | solution.py:423
  299.8 1.8 copy-start.2

commit v4 on v3

--- a/solution.py
+++ b/solution.py
@@ -228,7 +228,7 @@
 
 
 def weight_grads_kernel(cot, *refs):
-    halves, (out_ref, total) = (refs[0:5], refs[5:10]), refs[10:]
+    halves, total = (refs[0:5], refs[5:10]), refs[10]
     total[...] = jnp.zeros(total.shape, F32)
 
     def one(t, carry):
@@ -245,7 +245,6 @@
         return carry
 
     lax.fori_loop(0, cot.shape[0], one, 0)
-    pack(total, out_ref)
 
 
 def hidden_grad_kernel(one_ref, two_ref, cot_ref, out_ref, first_ref, last_ref):
@@ -261,9 +260,10 @@
         last_ref[f] = total[rows - 1]
 
 
-def conv_grad_kernel(top_ref, cells_ref, bottom_ref, grad_ref, out_ref, ext, pad, total):
+def conv_grad_kernel(top_ref, cells_ref, bottom_ref, grad_ref, others_ref, out_ref, ext, pad, total):
     frames, rows, cols, chans = cells_ref.shape
-    total[...] = jnp.zeros(total.shape, F32)
+    total[0:9] = jnp.zeros((9,) + total.shape[1:], F32)
+    total[9:] = others_ref[...]
 
     def one_frame(f, carry):
         ext[0] = top_ref[f]
@@ -286,7 +286,7 @@
     pack(total, out_ref)
 
 
-def hops(sizes, parts, links_first):
+def hops(sizes, parts):
     space, tm = sizes
     first, planes, line = [("space", 1)], [], []
     stride = 2
@@ -297,20 +297,15 @@
     while stride < tm:
         line.append(("tm", stride))
         stride *= 2
-    if links_first:
-        plan = [first + planes[p:] + planes[:p] + line for p in range(parts)]
-    else:
-        rest = planes + line
-        plan = [first + rest[p:] + rest[:p] for p in range(parts)]
+    rest = planes + line
+    plan = [first + rest[p:] + rest[:p] for p in range(parts)]
     return plan, first + planes + line
 
 
-def reduce_kernel(plan, greet, part_rows, beside, *refs):
-    if beside:
-        x_ref, top_ref, cells_ref, bottom_ref, weight_ref, out_ref, result_ref = refs[:7]
-        ext, pad, acc, low, send_sems, recv_sems, *recvs = refs[7:]
-    else:
-        x_ref, out_ref, acc, low, send_sems, recv_sems, *recvs = refs
+def reduce_kernel(plan, greet, part_rows, *refs):
+    x_ref, top_ref, cells_ref, bottom_ref, weight_ref, out_ref, result_ref = refs[:7]
+    ext, pad, acc, low, send_sems, recv_sems, *recvs = refs[7:]
+    frames, rows, cols, chans = cells_ref.shape
 
     def bit_and_partner(axis, stride):
         me = lax.axis_index(axis)
@@ -345,11 +340,9 @@
             )
             copy.start()
             copies.append(copy)
-        if beside:
-            frames, rows, cols, chans = cells_ref.shape
-            for f in range(s, frames, steps):
-                total = conv_frame(f, top_ref, cells_ref, bottom_ref, weight_ref, ext, pad)
-                result_ref[f] = total.astype(BF16).reshape(rows, cols, chans)
+        for f in range(s, frames, steps):
+            total = conv_frame(f, top_ref, cells_ref, bottom_ref, weight_ref, ext, pad)
+            result_ref[f] = total.astype(BF16).reshape(rows, cols, chans)
         for p in range(parts):
             copies[p].wait()
             acc[pl.ds(keeps[p], half)] = src[pl.ds(keeps[p], half)] + recvs[s][p]
@@ -379,21 +372,22 @@
     out_ref[...] = low[...]
 
 
-def unpack_kernel(norm, packed_ref, out_ref):
-    count, chans, _ = out_ref.shape
-    for row, lane, m, col, width in pack_places(count, chans)[0]:
-        piece = packed_ref[row : row + chans, lane : lane + width].astype(F32)
-        out_ref[m, :, col : col + width] = piece * norm
-
-
-def total_over_devices(arr, count, chans, norm, sizes, parts, part_rows, links_first, number, conv=()):
-    plan, greet = hops(sizes, parts, links_first)
+def unpack_kernel(norm, packed_ref, conv_ref, *refs):
+    chans = conv_ref.shape[-1]
+    taps = conv_ref.shape[0]
+    for row, lane, m, col, width in pack_places(taps + len(refs), chans)[0]:
+        piece = packed_ref[row : row + chans, lane : lane + width].astype(F32) * norm
+        if m < taps:
+            conv_ref[m, :, col : col + width] = piece
+        else:
+            refs[m - taps][:, col : col + width] = piece
+
+
+def total_over_devices(arr, chans, norm, sizes, parts, part_rows, conv):
+    plan, greet = hops(sizes, parts)
     steps = len(greet)
-    out = shape_of(arr.shape, BF16)
-    scratch = []
-    if conv:
-        out = (out, shape_of(conv[1].shape, BF16))
-        scratch += conv_scratch(*conv[1].shape[1:])
+    out = (shape_of(arr.shape, BF16), shape_of(conv[1].shape, BF16))
+    scratch = conv_scratch(*conv[1].shape[1:])
     scratch += [
         pltpu.VMEM(arr.shape, F32),
         pltpu.VMEM(arr.shape, BF16),
@@ -401,19 +395,20 @@
         pltpu.SemaphoreType.DMA((2 * steps, parts)),
     ]
     scratch += [pltpu.VMEM((parts, part_rows >> (s + 1), LANES), F32) for s in range(steps)]
-    result = call(
-        functools.partial(reduce_kernel, plan, greet, part_rows, bool(conv)),
+    packed, result = call(
+        functools.partial(reduce_kernel, plan, greet, part_rows),
         out,
         (arr,) + conv,
         scratch,
-        collective_id=number,
+        collective_id=0,
         has_side_effects=True,
     )
-    packed = result[0] if conv else result
     grads = call(
-        functools.partial(unpack_kernel, norm), shape_of((count, chans, chans), F32), (packed,)
-    )
-    return (grads, result[1]) if conv else grads
+        functools.partial(unpack_kernel, norm),
+        (shape_of((9, chans, chans), F32),) + (shape_of((chans, chans), F32),) * 4,
+        (packed,),
+    )
+    return grads, result
 
 
 def halo(first, last):
@@ -450,6 +445,7 @@
     cot_all = owned(cot_groups, per_source)
     weights = conv_weight.reshape(9, chans, chans)
     hidden = convolve(top, latents, bottom, weights, [tm * half for half in halves])
+    hidden, cot_all = lax.optimization_barrier((hidden, cot_all))
     backs, saved = [], []
     for i, half in enumerate(halves):
         hid = owned(hidden[i], half)
@@ -473,16 +469,12 @@
         )
         backs.append(exchange(attn_cols.reshape(tm * half, span, chans)))
         saved += [hid] + grads
-    small_rows = part_size(4, chans, 2, devices)
     small = call(
         weight_grads_kernel,
-        shape_of((2 * small_rows, LANES), F32),
+        shape_of((4, chans, chans), F32),
         (cot_all, *saved),
-        [pltpu.VMEM((4, chans, chans), F32)],
         flops=8 * cot_all.size * chans,
     )
-    small = total_over_devices(small, 4, chans, norm, sizes, 2, small_rows, True, 0)
-    backs, small = lax.optimization_barrier((backs, small))
     hidden_grad, first, last = call(
         hidden_grad_kernel,
         (
@@ -493,29 +485,25 @@
         (*backs, cotangent),
     )
     grad_top, grad_bottom = halo(first, last)
-    part_rows = part_size(9, chans, 3, devices)
-    conv_part = call(
+    part_rows = part_size(13, chans, 3, devices)
+    packed = call(
         conv_grad_kernel,
         shape_of((3 * part_rows, LANES), F32),
-        (top, latents, bottom, hidden_grad),
-        conv_scratch(rows, cols, chans) + [pltpu.VMEM((9, chans, chans), F32)],
+        (top, latents, bottom, hidden_grad, small),
+        conv_scratch(rows, cols, chans) + [pltpu.VMEM((13, chans, chans), F32)],
         flops=18 * latents.size * chans,
     )
     turned = jnp.swapaxes(conv_weight[::-1, ::-1], 2, 3).reshape(9, chans, chans)
-    grad_conv, grad_input = total_over_devices(
-        conv_part,
-        9,
+    (grad_conv, *others), grad_input = total_over_devices(
+        packed,
         chans,
         norm,
         sizes,
         3,
         part_rows,
-        False,
-        1,
         (grad_top, hidden_grad, grad_bottom, turned),
     )
-    grad_conv = grad_conv.reshape(3, 3, chans, chans)
-    return grad_input, grad_conv, small[0], small[1], small[2], small[3]
+    return grad_input, grad_conv.reshape(3, 3, chans, chans), *others
 
 
 def solution(mesh):

time: 305 us -> 263 us (0.86)
  Pallas kernels: 201 us -> 142 us
  blocking collectives: 29.8 us -> 44.6 us
  starting transfers between devices: 27.4 us -> 21.5 us
  waiting for transfers between devices: 12.9 us -> 17.7 us
    pallas_call x11 -> x9, Pallas kernels: 201 us -> 142 us  [call(): pl.pallas_call(body, out_shape=out_shape, in_specs=[pl.BlockSpec(memory_s...]
    all_to_all x1 -> x2, blocking collectives: 29.8 us -> 44.6 us  [exchange(): return lax.all_to_all(arr, 'tm', split_axis=0, concat_axis=0, tiled=True)]
    all_to_all x4 -> x3, waiting for transfers between devices: 11.9 us -> 17.3 us  [exchange(): return lax.all_to_all(arr, 'tm', split_axis=0, concat_axis=0, tiled=True)]
    all_to_all x4 -> x3, starting transfers between devices: 19.1 us -> 14.3 us  [exchange(): return lax.all_to_all(arr, 'tm', split_axis=0, concat_axis=0, tiled=True)]
    unnamed x57 -> x61, local copies, waits for them, and re-layouts: 14.9 us -> 19 us
  transfers between devices with their start and end apart: 8 -> 7, of which waited for: 3 -> 3; matrix products, arithmetic and copies ran while one was open for 6% -> 5% of each run, Pallas kernels for 39% -> 24%
where the time goes in v4:
time: 263 us; the launch traced here: 261 us
  Pallas kernels  142 us (54%)
  blocking collectives  44.6 us (17%)
  local copies, waits for them, and re-layouts  34.7 us (13%)
  starting transfers between devices  21.5 us (8%)
  waiting for transfers between devices  17.7 us (7%)
    pallas_call x9, Pallas kernels, call(): pl.pallas_call(body, out_shape=out_shape, in_specs=[pl.BlockSpec(memory_s...  142 us
    all_to_all x2, blocking collectives, exchange(): return lax.all_to_all(arr, 'tm', split_axis=0, concat_axis=0, tiled=True)  44.6 us
    unnamed x61, local copies, waits for them, and re-layouts  19 us
    all_to_all x3, waiting for transfers between devices, exchange(): return lax.all_to_all(arr, 'tm', split_axis=0, concat_axis=0, tiled=True)  17.3 us
    all_to_all x3, starting transfers between devices, exchange(): return lax.all_to_all(arr, 'tm', split_axis=0, concat_axis=0, tiled=True)  14.3 us
    transpose x2, local copies, waits for them, and re-layouts, on_device(): jnp.swapaxes(conv_weight[::-1, ::-1], 2, 3).reshape(9, chans, chans)  7.58 us
    ppermute x4, starting transfers between devices, halo(): return (lax.ppermute(last, 'space', up), lax.ppermute(first, 'space', down))  7.22 us
  transfers between devices with their start and end apart: 7, of which 3 were waited for; matrix products, arithmetic and copies ran while one was open for 5% of the time, Pallas kernels for 24%

profile of v4, /device:TPU:0, one launch (start us, length us, event | category | flops | bytes accessed | tf_op | source)
XLA Modules:
  0.0 261.1 jit_solution(16534751058466355585)
XLA Ops:
  0.6 1.8 copy.30.cells_ref.cot_ref
  2.5 0.0 copy-start
  2.5 1.3 shard_map.119
  3.8 0.2 copy-done
  4.0 6.4 %all-to-all-start = ((bf16[60,32,320]{2,1,0:T(8,128)(2,1)}), bf16[60,32,320]{2,1,0:T(8,128)(2,1)}, u32[]{:S(2)}, u32[]{:S(2)}) async-start(bf16[60,32,320]{2,1,0:T(8,128)(2,1)} %shard_map.119), calls=%async_computation | async-start | bytes 2949120 | tf_op jit(solution)/shard_map/all_to_all | solution.py:434
  10.5 0.1 slice_bitcast_fusion
  10.6 2.3 collective-permute-start
  12.9 1.3 collective-permute-start.1
  14.2 1.6 copy.37.cells_ref
  15.7 0.0 collective-permute-done
  15.7 1.4 copy.36.top_ref
  17.2 0.4 collective-permute-done.1
  17.6 0.4 copy.38.bottom_ref
  18.0 12.2 %shard_map.118 = (bf16[32,32,320]{2,1,0:T(8,128)(2,1)}, bf16[28,32,320]{2,1,0:T(8,128)(2,1)S(1)}) custom-call(bf16[4,240,320]{2,1,0:T(8,128)(2,1)S(1)} %copy.36.top_ref, bf16[4,2,240,320]{3,2,1,0:T(8,128)(2,1)} %copy.37.cells_ref, bf16[4,240,320]{2,1,0:T(8,128)(2,1)S(1)} %copy.38.bottom_ref, bf16[9,320,320]{2,1,0:T(8,128)(2,1)} %bitcast.34), custom_call_target="tpu_custom_call" | custom-call | flops 3538944000 | bytes 8601600 | tf_op jit(solution)/shard_map/pallas_call | solution.py:21
  30.1 15.3 %all-to-all-done = bf16[60,32,320]{2,1,0:T(8,128)(2,1)} async-done(((bf16[60,32,320]{2,1,0:T(8,128)(2,1)}), bf16[60,32,320]{2,1,0:T(8,128)(2,1)}, u32[]{:S(2)}, u32[]{:S(2)}) %all-to-all-start) | async-done | bytes 1228832 | tf_op jit(solution)/shard_map/all_to_all | solution.py:434
  45.4 20.7 %all_to_all.25 = bf16[28,32,320]{2,1,0:T(8,128)(2,1)} all-to-all(bf16[28,32,320]{2,1,0:T(8,128)(2,1)S(1)} %get-tuple-element.36), channel_id=1, replica_groups=mesh['space'=8,'tm'=4] {'tm'}, dimensions={0} | all-to-all | bytes 1146880 | tf_op jit(solution)/shard_map/all_to_all | solution.py:434
  66.2 4.3 %all-to-all-start.1 = ((bf16[32,32,320]{2,1,0:T(8,128)(2,1)}), bf16[32,32,320]{2,1,0:T(8,128)(2,1)}, u32[]{:S(2)}, u32[]{:S(2)}) async-start(bf16[32,32,320]{2,1,0:T(8,128)(2,1)} %get-tuple-element.33), calls=%async_computation.1 | async-start | bytes 1572864 | tf_op jit(solution)/shard_map/all_to_all | solution.py:434
  70.5 0.2 copy.31
  70.7 0.0 copy-done.13
  70.8 0.0 copy-start.17
  70.8 0.2 copy.32
  71.0 0.0 copy-done.14
  71.0 0.0 copy-start.19
  71.0 0.2 copy.33
  71.2 0.0 copy-start.21
  71.2 0.2 copy.34
  71.4 0.0 copy-start.23
  71.4 14.5 %shard_map.121 = (bf16[4,7,32,320]{3,2,1,0:T(8,128)(2,1)}, bf16[4,7,32,320]{3,2,1,0:T(8,128)(2,1)S(1)}, bf16[4,7,32,320]{3,2,1,0:T(8,128)(2,1)S(1)}, bf16[4,7,32...) custom-call(bf16[4,7,32,320]{3,2,1,0:T(8,128)(2,1)} %bitcast.22, bf16[4,15,32,320]{3,2,1,0:T(8,128)(2,1)} %bitcast.3.cot, ...), custom_call_target="tpu_custom_call" | custom-call | flops 1835008000 | bytes 6471680 | tf_op jit(solution)/shard_map/pallas_call | solution.py:21
  86.0 0.9 copy-done.7
  86.8 0.9 copy-done.9
  87.7 2.0 all-to-all-done.1
  89.6 3.5 %all-to-all-start.4 = ((bf16[28,32,320]{2,1,0:T(8,128)(2,1)}), bf16[28,32,320]{2,1,0:T(8,128)(2,1)S(1)}, u32[]{:S(2)}, u32[]{:S(2)}) async-start(bf16[28,32,320]{2,1,0:T(8,128)(2,1)} %bitcast.11), calls=%async_computation.4 | async-start | bytes 1376256 | tf_op jit(solution)/shard_map/all_to_all | solution.py:434
  93.1 0.0 copy-start.16
  93.2 0.9 copy-done.16
  94.1 0.9 copy-done.18
  95.0 0.9 copy-done.20
  96.0 0.9 copy-done.22
  96.9 0.9 copy-done.24
  97.9 15.5 %shard_map.120 = (bf16[4,8,32,320]{3,2,1,0:T(8,128)(2,1)S(1)}, bf16[4,8,32,320]{3,2,1,0:T(8,128)(2,1)S(1)}, bf16[4,8,32,320]{3,2,1,0:T(8,128)(2,1)S(1)}, bf16[4,...) custom-call(bf16[4,8,32,320]{3,2,1,0:T(8,128)(2,1)} %bitcast.4.hid.refs_0_, bf16[4,15,32,320]{3,2,1,0:T(8,128)(2,1)} %bitcast.3.cot, ...), custom_call_target="tpu_custom_call" | custom-call | flops 2097152000 | bytes 6635520 | tf_op jit(solution)/shard_map/pallas_call | solution.py:21
  113.3 0.9 copy-done.4
  114.2 0.9 copy-done.5
  115.1 0.0 all-to-all-done.4.two_ref
  115.1 23.9 %all_to_all.26.one_ref = bf16[32,32,320]{2,1,0:T(8,128)(2,1)S(1)} all-to-all(bf16[32,32,320]{2,1,0:T(8,128)(2,1)S(1)} %bitcast.24), channel_id=1, replica_groups=mesh['space'=8,'tm'=4] {'tm'}, dimensions={0} | all-to-all | bytes 1310720 | tf_op jit(solution)/shard_map/all_to_all | solution.py:434
  139.0 2.8 %shard_map.122 = (bf16[4,2,240,320]{3,2,1,0:T(8,128)(2,1)}, bf16[4,240,320]{2,1,0:T(8,128)(2,1)S(1)}, bf16[4,240,320]{2,1,0:T(8,128)(2,1)S(1)}) custom-call(bf16[32,32,320]{2,1,0:T(8,128)(2,1)S(1)} %all_to_all.26.one_ref, bf16[28,32,320]{2,1,0:T(8,128)(2,1)S(1)} %all-to-all-done.4.two_ref, bf16[4,2,240,320]{3,2,1,0:T(8,128)(2,1)} %copy-done), custom_call_target="tpu_custom_call" | custom-call | bytes 4915200 | tf_op jit(solution)/shard_map/pallas_call | solution.py:21
  141.8 0.9 copy-done.6
  142.7 2.2 copy.39
  144.9 2.2 collective-permute-start.2
  147.1 1.1 copy.40
  148.2 1.5 collective-permute-start.3
  149.7 3.2 %reverse_bitcast_fusion = bf16[3,3,320,320]{2,3,1,0:T(8,128)(2,1)} fusion(bf16[3,3,320,320]{3,2,1,0:T(8,128)(2,1)} %param.9), kind=kLoop, calls=%fused_computation | loop fusion | bytes 3686400 | tf_op jit(solution)/shard_map/transpose | solution.py:496
  152.9 4.4 %copy.41 = bf16[3,3,320,320]{3,2,1,0:T(8,128)(2,1)} copy(bf16[3,3,320,320]{2,3,1,0:T(8,128)(2,1)} %reverse_bitcast_fusion) | data formatting | bytes 3686400 | tf_op jit(solution)/shard_map/transpose | solution.py:496
  157.3 0.0 copy-done.8
  157.3 1.1 copy-done.11
  158.4 1.1 copy-done.12
  159.5 7.6 %shard_map.123.others_ref = f32[4,320,320]{2,1,0:T(8,128)} custom-call(bf16[4,15,32,320]{3,2,1,0:T(8,128)(2,1)} %bitcast.3.cot, bf16[4,8,32,320]{3,2,1,0:T(8,128)(2,1)} %bitcast.4.hid.refs_0_, bf16[4,8,32,320]{3,2,1,0:T(8,128)(2,1)} %copy-done.4, bf16[4,8,32,320]{3,2,1,0:T(8,128)(2,1)} %copy-done.5, bf16[4,8,32,320]{3,2,1,0:T(8,128)(2,1)} %get-tuple-element.41.refs_3_, ...), custom_call_target="tpu_custom_call" | custom-call | flops 1572864000 | bytes 14745600 | tf_op jit(solution)/shard_map/pallas_call | solution.py:21
  167.1 12.6 %shard_map.124.refs_0_ = f32[10752,128]{1,0:T(8,128)} custom-call(bf16[4,240,320]{2,1,0:T(8,128)(2,1)S(1)} %copy.36.top_ref, bf16[4,2,240,320]{3,2,1,0:T(8,128)(2,1)S(1)} %copy-done.3, bf16[4,240,320]{2,1,0:T(8,128)(2,1)S(1)} %copy.38.bottom_ref, bf16[4,2,240,320]{3,2,1,0:T(8,128)(2,1)} %get-tuple-element.38.grad_ref.refs_2_, ...), custom_call_target="tpu_custom_call" | custom-call | flops 3538944000 | bytes 10649600 | tf_op jit(solution)/shard_map/pallas_call | solution.py:21
  179.6 0.0 collective-permute-done.2
  179.6 1.4 copy.42.refs_1_
  181.1 0.0 collective-permute-done.3
  181.1 1.4 copy.43.refs_3_
  182.5 72.3 %shard_map.125 = (bf16[10752,128]{1,0:T(8,128)(2,1)}, bf16[4,2,240,320]{3,2,1,0:T(8,128)(2,1)S(1)}) custom-call(f32[10752,128]{1,0:T(8,128)} %shard_map.124.refs_0_, bf16[4,240,320]{2,1,0:T(8,128)(2,1)S(1)} %copy.42.refs_1_, bf16[4,2,240,320]{3,2,1,0:T(8,128)(2,1)} %get-tuple-element.38.grad_ref.refs_2_, bf16[4,240,320]{2,1,0:T(8,128)(2,1)S(1)} %copy.43.refs_3_, ...), custom_call_target="tpu_custom_call" | custom-call | bytes 19611648 | tf_op jit(solution)/shard_map/pallas_call | solution.py:21
  254.8 1.8 copy-done.1
  256.6 3.0 %shard_map.126 = (f32[9,320,320]{2,1,0:T(8,128)}, f32[320,320]{1,0:T(8,128)}, f32[320,320]{1,0:T(8,128)}, f32[320,320]{1,0:T(8,128)}, f32[320,320]{1,0:T(8,128)}) custom-call(bf16[10752,128]{1,0:T(8,128)(2,1)S(1)} %copy-done.1), custom_call_target="tpu_custom_call" | custom-call | bytes 5505024 | tf_op jit(solution)/shard_map/pallas_call | solution.py:21
  259.6 1.6 copy.44
  (31 shorter events, 0.1 us)
Async XLA Ops:
  2.5 1.6 copy-start
  4.0 6.5 %copy-start.25 = (bf16[4,2,240,320]{2,3,1,0:T(8,128)(2,1)S(1)}, bf16[4,2,240,320]{2,3,1,0:T(8,128)(2,1)}, u32[]{:S(2)}) copy-start(bf16[4,2,240,320]{2,3,1,0:T(8,128)(2,1)} %param.7) | copy-start | bytes 3686404
  4.0 41.4 %all-to-all-start = ((bf16[60,32,320]{2,1,0:T(8,128)(2,1)}), bf16[60,32,320]{2,1,0:T(8,128)(2,1)}, u32[]{:S(2)}, u32[]{:S(2)}) async-start(bf16[60,32,320]{2,1,0:T(8,128)(2,1)} %shard_map.119), calls=%async_computation | async-start | bytes 2949120 | tf_op jit(solution)/shard_map/all_to_all | solution.py:434
  10.6 5.2 %collective-permute-start = (bf16[4,240,320]{1,2,0:T(8,128)(2,1)S(1)}, bf16[4,240,320]{1,2,0:T(8,128)(2,1)}, u32[]{:S(2)}, u32[]{:S(2)}) collective-permute-start(bf16[4,240,320]{1,2,0:T(8,128)(2,1)S(1)} %get-tuple-element.69), channel_id=1, source_target_pairs={{0,4},{4,8},{8,12},{12,16},{16,20},{20,24},{24,28},{1,5},{5,9},{9,... | collective-permute-start | bytes 1843208 | tf_op jit(solution)/shard_map/ppermute | solution.py:418
  12.9 4.7 %collective-permute-start.1 = (bf16[4,240,320]{1,2,0:T(8,128)(2,1)S(1)}, bf16[4,240,320]{1,2,0:T(8,128)(2,1)S(1)}, u32[]{:S(2)}, u32[]{:S(2)}) collective-permute-start(bf16[4,240,320]{1,2,0:T(8,128)(2,1)S(1)} %get-tuple-element.68), channel_id=1, source_target_pairs={{4,0},{8,4},{12,8},{16,12},{20,16},{24,20},{28,24},{5,1},{9,5},{13... | collective-permute-start | bytes 1843208 | tf_op jit(solution)/shard_map/ppermute | solution.py:418
  45.4 25.1 %copy-start.26 = (bf16[320,320]{1,0:T(8,128)(2,1)S(1)}, bf16[320,320]{1,0:T(8,128)(2,1)}, u32[]{:S(2)}) copy-start(bf16[320,320]{1,0:T(8,128)(2,1)} %param.13) | copy-start | bytes 614404
  45.4 25.3 %copy-start.13 = (bf16[320,320]{1,0:T(8,128)(2,1)S(1)}, bf16[320,320]{1,0:T(8,128)(2,1)}, u32[]{:S(2)}) copy-start(bf16[320,320]{1,0:T(8,128)(2,1)} %wq.3) | copy-start | bytes 614404
  66.2 4.8 %copy-start.14 = (bf16[320,320]{1,0:T(8,128)(2,1)S(1)}, bf16[320,320]{1,0:T(8,128)(2,1)}, u32[]{:S(2)}) copy-start(bf16[320,320]{1,0:T(8,128)(2,1)} %wk.3) | copy-start | bytes 614404
  66.2 5.0 %copy-start.15 = (bf16[320,320]{1,0:T(8,128)(2,1)S(1)}, bf16[320,320]{1,0:T(8,128)(2,1)}, u32[]{:S(2)}) copy-start(bf16[320,320]{1,0:T(8,128)(2,1)} %wv.3) | copy-start | bytes 614404
  66.2 23.5 %all-to-all-start.1 = ((bf16[32,32,320]{2,1,0:T(8,128)(2,1)}), bf16[32,32,320]{2,1,0:T(8,128)(2,1)}, u32[]{:S(2)}, u32[]{:S(2)}) async-start(bf16[32,32,320]{2,1,0:T(8,128)(2,1)} %get-tuple-element.33), calls=%async_computation.1 | async-start | bytes 1572864 | tf_op jit(solution)/shard_map/all_to_all | solution.py:434
  70.8 15.2 %copy-start.17 = (bf16[320,320]{0,1:T(8,128)(2,1)}, bf16[320,320]{0,1:T(8,128)(2,1)S(1)}, u32[]{:S(2)}) copy-start(bf16[320,320]{0,1:T(8,128)(2,1)S(1)} %copy.31) | copy-start | bytes 614404
  71.0 15.0 %copy-start.19 = (bf16[320,320]{0,1:T(8,128)(2,1)}, bf16[320,320]{0,1:T(8,128)(2,1)S(1)}, u32[]{:S(2)}) copy-start(bf16[320,320]{0,1:T(8,128)(2,1)S(1)} %copy.32) | copy-start | bytes 614404
  71.2 14.7 %copy-start.21 = (bf16[320,320]{0,1:T(8,128)(2,1)}, bf16[320,320]{0,1:T(8,128)(2,1)S(1)}, u32[]{:S(2)}) copy-start(bf16[320,320]{0,1:T(8,128)(2,1)S(1)} %copy.33) | copy-start | bytes 614404
  71.4 14.5 %copy-start.23 = (bf16[320,320]{0,1:T(8,128)(2,1)}, bf16[320,320]{0,1:T(8,128)(2,1)S(1)}, u32[]{:S(2)}) copy-start(bf16[320,320]{0,1:T(8,128)(2,1)S(1)} %copy.34) | copy-start | bytes 614404
  85.9 0.9 copy-start.7
  86.8 0.9 copy-start.9
  89.6 25.5 %all-to-all-start.4 = ((bf16[28,32,320]{2,1,0:T(8,128)(2,1)}), bf16[28,32,320]{2,1,0:T(8,128)(2,1)S(1)}, u32[]{:S(2)}, u32[]{:S(2)}) async-start(bf16[28,32,320]{2,1,0:T(8,128)(2,1)} %bitcast.11), calls=%async_computation.4 | async-start | bytes 1376256 | tf_op jit(solution)/shard_map/all_to_all | solution.py:434
  93.1 0.9 copy-start.16
  94.1 0.9 copy-start.18
  95.0 0.9 copy-start.20
  96.0 0.9 copy-start.22
  96.9 0.9 copy-start.24
  113.3 0.9 copy-start.4
  114.2 0.9 copy-start.5
  141.8 0.9 copy-start.6
  144.9 34.7 %collective-permute-start.2 = (bf16[4,240,320]{1,2,0:T(8,128)(2,1)}, bf16[4,240,320]{1,2,0:T(8,128)(2,1)}, u32[]{:S(2)}, u32[]{:S(2)}) collective-permute-start(bf16[4,240,320]{1,2,0:T(8,128)(2,1)} %copy.39), channel_id=1, source_target_pairs={{0,4},{4,8},{8,12},{12,16},{16,20},{20,24},{24,28},{1,5},{5,9},{9,... | collective-permute-start | bytes 1843208 | tf_op jit(solution)/shard_map/ppermute | solution.py:418
  148.2 32.9 %collective-permute-start.3 = (bf16[4,240,320]{1,2,0:T(8,128)(2,1)}, bf16[4,240,320]{1,2,0:T(8,128)(2,1)}, u32[]{:S(2)}, u32[]{:S(2)}) collective-permute-start(bf16[4,240,320]{1,2,0:T(8,128)(2,1)} %copy.40), channel_id=1, source_target_pairs={{4,0},{8,4},{12,8},{16,12},{20,16},{24,20},{28,24},{5,1},{9,5},{13... | collective-permute-start | bytes 1843208 | tf_op jit(solution)/shard_map/ppermute | solution.py:418
  152.9 4.4 %copy-start.2 = (bf16[28,32,320]{2,1,0:T(8,128)(2,1)S(1)}, bf16[28,32,320]{2,1,0:T(8,128)(2,1)}, u32[]{:S(2)}) copy-start(bf16[28,32,320]{2,1,0:T(8,128)(2,1)} %all_to_all.25) | copy-start | bytes 1720324
  152.9 4.4 %copy-start.8 = (bf16[4,7,32,320]{3,2,1,0:T(8,128)(2,1)S(1)}, bf16[4,7,32,320]{3,2,1,0:T(8,128)(2,1)}, u32[]{:S(2)}) copy-start(bf16[4,7,32,320]{3,2,1,0:T(8,128)(2,1)} %copy-done.7) | copy-start | bytes 1720324
  152.9 4.4 %copy-start.10 = (bf16[4,7,32,320]{3,2,1,0:T(8,128)(2,1)S(1)}, bf16[4,7,32,320]{3,2,1,0:T(8,128)(2,1)}, u32[]{:S(2)}) copy-start(bf16[4,7,32,320]{3,2,1,0:T(8,128)(2,1)} %copy-done.9) | copy-start | bytes 1720324
  157.3 1.1 copy-start.11
  158.4 1.1 copy-start.12
  159.5 7.6 %copy-start.3 = (bf16[4,2,240,320]{3,2,1,0:T(8,128)(2,1)S(1)}, bf16[4,2,240,320]{3,2,1,0:T(8,128)(2,1)}, u32[]{:S(2)}) copy-start(bf16[4,2,240,320]{3,2,1,0:T(8,128)(2,1)} %copy.37.cells_ref) | copy-start | bytes 3686404
  254.8 1.8 copy-start.1
